TPU v7x, 32 devices: a whole 2x2x4 slice. The times are simulated.
32 devices in a mesh: wide: 8 (over z, x), narrow: 4 (over y, core).
Axes of the slice: x: 2, y: 2, z: 4, core: 2. Of those that a mesh axis runs over, the one named last changes fastest.
Arguments:
- inputs: bfloat16 [16384, 1024], P('wide', 'narrow'), may hold values from -6 to 6
- cotangent: bfloat16 [16384, 1024], P('wide', 'narrow'), may hold values from -6 to 6
- lengths: int32 [8], P('wide'), may hold values from 213 to 1024, as said below
- ln_gain: float32 [1024], replicated, may hold values from 0.5 to 1.5
- ln_bias: float32 [1024], replicated, may hold values from -3 to 3
- w_qkv: bfloat16 [1024, 3072], replicated, may hold values from -0.1875 to 0.1875
- w_out: bfloat16 [1024, 1024], replicated, may hold values from -3 to 3
- w_in: bfloat16 [1024, 4096], P(None, 'narrow'), may hold values from -0.1875 to 0.1875
- b_in: float32 [4096], P('narrow'), may hold values from -3 to 3
- w_down: bfloat16 [4096, 1024], P('narrow'), may hold values from -0.09375 to 0.09375
- b_down: float32 [1024], P('narrow'), may hold values from -3 to 3
Outputs:
- mixed: bfloat16 [16384, 1024], P('wide', 'narrow')
- g_inputs: float32 [16384, 1024], P('wide', 'narrow')
- g_ln_gain: float32 [1024], P('narrow')
- g_ln_bias: float32 [1024], P('narrow')
- g_w_qkv: float32 [1024, 3, 1024], P('wide', None, 'narrow')
- g_w_out: float32 [1024, 1024], P('narrow', 'wide')
- g_w_in: float32 [1024, 4096], P('wide', 'narrow')
- g_b_in: float32 [4096], P('narrow')
- g_w_down: float32 [4096, 1024], P('narrow', 'wide')
- g_b_down: float32 [1024], P('narrow')
Inputs may be any that keep to these rules, and one draw needn't show every extreme that they name: `lengths`: both rows of a pair have this length; positions at or past it are padding. The longest length in all is exactly 1024.
All inputs are finite; a program needn't handle non-finite values.
Results may differ from a plain program's by a relative error of at most 0.0096.
Values may be sent and summed in bfloat16 or wider, within the bound.
No kernel may reach another device: no remote copies, remote signals or barrier semaphores. Data moves between devices by JAX's collectives and lax.ppermute only.
A program may use at most 384 MiB of HBM per device.

v0:
```python
import jax
import jax.numpy as jnp
from jax import lax
from jax.sharding import PartitionSpec as P

HEAD_DIM = 64
ROT = 32


norm_eps = 1e-05


def gelu_tanh(value_in):
    return (
        0.5
        * value_in
        * (
            1.0
            + jnp.tanh(0.7978845608028654 * (value_in + 0.044715 * value_in * value_in * value_in))
        )
    )


def rotary_tables(seq_len, rot_dims):
    position = jnp.arange(seq_len).astype(jnp.float32)[:, None]
    freq_index = jnp.arange(rot_dims // 2).astype(jnp.float32)[None, :]
    angles = position * 10000.0 ** (-2.0 * freq_index / rot_dims)
    return (jnp.cos(angles), jnp.sin(angles))


def rotate(field_in, cosine, sine_table, rot_dims):
    rotated = field_in[..., :rot_dims]
    others = field_in[..., rot_dims:]
    pair_view = rotated.reshape(rotated.shape[:-1] + (rot_dims // 2, 2))
    first_half = pair_view[..., 0]
    second_half = pair_view[..., 1]
    cos_table = cosine[:, None, :]
    sin_table = sine_table[:, None, :]
    new_first = first_half * cos_table - second_half * sin_table
    new_second = second_half * cos_table + first_half * sin_table
    joined = jnp.stack([new_first, new_second], axis=-1).reshape(rotated.shape)
    return jnp.concatenate([joined, others], axis=-1)


def causal_mask(first_row, block_rows, last_row, length):
    query_pos = first_row + jnp.arange(block_rows)[:, None]
    key_pos = jnp.arange(last_row)[None, :]
    return (key_pos <= query_pos) & (key_pos < length)


def block_scores(queries, key_rows, first_row, last_row, length):
    score_scale = HEAD_DIM ** (-0.5)
    scores = (
        jnp.einsum(
            "qhd,khd->hqk",
            queries[first_row:last_row],
            key_rows[:last_row],
            preferred_element_type=jnp.float32,
        )
        * score_scale
    )
    allowed = causal_mask(first_row, last_row - first_row, last_row, length)
    return jnp.where(allowed[None], scores, -1e30)


def attend_forward(queries, key_rows, values, length, block_rows):
    seq_len = queries.shape[0]
    queries = queries.reshape(seq_len, -1, HEAD_DIM)
    key_rows = key_rows.reshape(seq_len, -1, HEAD_DIM)
    values = values.reshape(seq_len, -1, HEAD_DIM)
    outputs = []
    lse_parts = []
    for first_row in range(0, seq_len, block_rows):
        last_row = first_row + block_rows
        scores = block_scores(queries, key_rows, first_row, last_row, length)
        row_max = jnp.max(scores, axis=-1, keepdims=True)
        exp_scores = jnp.exp(scores - row_max)
        row_total = jnp.sum(exp_scores, axis=-1, keepdims=True)
        probs_low = (exp_scores / row_total).astype(jnp.bfloat16)
        outputs.append(
            jnp.einsum(
                "hqk,khd->qhd", probs_low, values[:last_row], preferred_element_type=jnp.float32
            )
        )
        lse_parts.append((row_max + jnp.log(row_total))[..., 0])
    return (
        jnp.concatenate(outputs, axis=0).reshape(seq_len, -1),
        jnp.concatenate(lse_parts, axis=1),
    )


def attend_backward(queries, key_rows, values, grad_att, lse_rows, length, block_rows):
    seq_len = queries.shape[0]
    score_scale = HEAD_DIM ** (-0.5)
    queries = queries.reshape(seq_len, -1, HEAD_DIM)
    key_rows = key_rows.reshape(seq_len, -1, HEAD_DIM)
    values = values.reshape(seq_len, -1, HEAD_DIM)
    grad_att = grad_att.reshape(seq_len, -1, HEAD_DIM)
    key_grads = jnp.zeros(key_rows.shape, jnp.float32)
    value_grads = jnp.zeros(values.shape, jnp.float32)
    query_grads = []
    for first_row in range(0, seq_len, block_rows):
        last_row = first_row + block_rows
        scores = block_scores(queries, key_rows, first_row, last_row, length)
        probs = jnp.exp(scores - lse_rows[:, first_row:last_row, None])
        probs_low = probs.astype(jnp.bfloat16)
        grad_block = grad_att[first_row:last_row]
        grad_probs = jnp.einsum(
            "qhd,khd->hqk", grad_block, values[:last_row], preferred_element_type=jnp.float32
        )
        row_inner = jnp.sum(probs * grad_probs, axis=-1, keepdims=True)
        grad_scores = (probs * (grad_probs - row_inner)).astype(jnp.bfloat16)
        query_grads.append(
            jnp.einsum(
                "hqk,khd->qhd", grad_scores, key_rows[:last_row], preferred_element_type=jnp.float32
            )
            * score_scale
        )
        key_grads = key_grads.at[:last_row].add(
            jnp.einsum(
                "hqk,qhd->khd",
                grad_scores,
                queries[first_row:last_row],
                preferred_element_type=jnp.float32,
            )
            * score_scale
        )
        value_grads = value_grads.at[:last_row].add(
            jnp.einsum("hqk,qhd->khd", probs_low, grad_block, preferred_element_type=jnp.float32)
        )
    return (jnp.concatenate(query_grads, axis=0), key_grads, value_grads)


def on_device(
    inputs, cotangent, lengths, ln_gain, ln_bias, w_qkv, w_out, w_in, b_in, w_down, b_down
):
    groups = lax.axis_size("wide")
    narrow_size = lax.axis_size("narrow")
    column = lax.axis_index("narrow")
    seq_count = 2 * lengths.shape[0]
    rows_all = inputs.shape[0]
    pad_len = rows_all // seq_count
    model_width = w_qkv.shape[0]
    share_cols = model_width // narrow_size
    block_rows = min(512, pad_len)
    col_start = column * share_cols
    token_count = 2.0 * jnp.sum(lengths.astype(jnp.float32))
    token_sum = lax.psum(token_count, "wide")
    group_scale = groups * token_count / token_sum
    full_x, full_cot = (
        lax.all_gather(inputs, "narrow", axis=1, tiled=True),
        lax.all_gather(cotangent, "narrow", axis=1, tiled=True),
    )
    seq_lengths = jnp.repeat(lengths, 2)
    valid_rows = (
        (jnp.arange(pad_len)[None, :] < seq_lengths[:, None])
        .astype(jnp.float32)
        .reshape(rows_all, 1)
    )
    x_full = full_x.astype(jnp.float32)
    row_mean = jnp.mean(x_full, axis=-1, keepdims=True)
    centered = x_full - row_mean
    inv_std = lax.rsqrt(jnp.mean(centered * centered, axis=-1, keepdims=True) + norm_eps)
    x_hat = centered * inv_std
    hidden = (x_hat * ln_gain + ln_bias).astype(jnp.bfloat16)
    qkv_proj = jnp.dot(hidden, w_qkv, preferred_element_type=jnp.float32)
    qkv_proj = qkv_proj.reshape(seq_count, pad_len, 3, -1, HEAD_DIM)
    cosine, sine_table = rotary_tables(pad_len, ROT)
    q_seq = (
        rotate(qkv_proj[:, :, 0], cosine, sine_table, ROT)
        .astype(jnp.bfloat16)
        .reshape(seq_count, pad_len, -1)
    )
    k_seq = (
        rotate(qkv_proj[:, :, 1], cosine, sine_table, ROT)
        .astype(jnp.bfloat16)
        .reshape(seq_count, pad_len, -1)
    )
    v_seq = qkv_proj[:, :, 2].astype(jnp.bfloat16).reshape(seq_count, pad_len, -1)
    att_width = q_seq.shape[2]
    up_proj = jnp.dot(hidden, w_in, preferred_element_type=jnp.float32) + b_in
    activation = gelu_tanh(up_proj).astype(jnp.bfloat16)
    mlp_part = jnp.dot(activation, w_down, preferred_element_type=jnp.float32)

    def forward_one(packed):
        return attend_forward(packed[0], packed[1], packed[2], packed[3], block_rows)

    att_rows, lse_all = lax.map(forward_one, (q_seq, k_seq, v_seq, seq_lengths))
    attended = att_rows.astype(jnp.bfloat16).reshape(rows_all, att_width)
    branch_share = lax.psum_scatter(
        mlp_part.astype(jnp.bfloat16), "narrow", scatter_dimension=1, tiled=True
    ).astype(jnp.float32)
    w_out_cols = lax.dynamic_slice_in_dim(w_out, col_start, share_cols, 1)
    attn_share = jnp.dot(attended, w_out_cols, preferred_element_type=jnp.float32)
    mixed = (inputs.astype(jnp.float32) + (attn_share + (branch_share + b_down))).astype(
        jnp.bfloat16
    )
    grad_share = group_scale * valid_rows * cotangent.astype(jnp.float32)
    grad_share_low = grad_share.astype(jnp.bfloat16)
    grad_low = (group_scale * valid_rows * full_cot.astype(jnp.float32)).astype(jnp.bfloat16)
    g_b_down = jnp.sum(grad_share_low.astype(jnp.float32), axis=0)
    g_w_down = jnp.einsum("rf,rd->fd", activation, grad_low, preferred_element_type=jnp.float32)
    g_act = jnp.dot(grad_low, w_down.T, preferred_element_type=jnp.float32)
    gelu_value, gelu_pull = jax.vjp(gelu_tanh, up_proj)
    g_up = gelu_pull(g_act)[0].astype(jnp.bfloat16)
    g_b_in = jnp.sum(g_up.astype(jnp.float32), axis=0)
    g_w_in = jnp.einsum("rd,rf->df", hidden, g_up, preferred_element_type=jnp.float32)
    g_hidden_mlp = jnp.dot(g_up, w_in.T, preferred_element_type=jnp.float32)
    g_w_out_rows = jnp.einsum("rd,re->de", attended, grad_low, preferred_element_type=jnp.float32)
    g_att = jnp.dot(grad_low, w_out.T, preferred_element_type=jnp.float32).astype(jnp.bfloat16)

    def backward_one(packed):
        return attend_backward(
            packed[0], packed[1], packed[2], packed[3], packed[4], packed[5], block_rows
        )

    g_qrot, g_krot, g_val = lax.map(
        backward_one,
        (q_seq, k_seq, v_seq, g_att.reshape(seq_count, pad_len, att_width), lse_all, seq_lengths),
    )
    g_query = rotate(g_qrot, cosine, -sine_table, ROT)
    g_key = rotate(g_krot, cosine, -sine_table, ROT)
    g_qkv = (
        jnp.stack([g_query, g_key, g_val], axis=2)
        .reshape(rows_all, 3 * att_width)
        .astype(jnp.bfloat16)
    )
    g_w_qkv = jnp.einsum("rd,rc->dc", hidden, g_qkv, preferred_element_type=jnp.float32)
    g_hidden_attn = jnp.dot(g_qkv, w_qkv.T, preferred_element_type=jnp.float32)
    g_hidden = g_hidden_attn + lax.psum(g_hidden_mlp.astype(jnp.bfloat16), "narrow").astype(
        jnp.float32
    )
    d_hat = g_hidden * ln_gain
    g_x_full = inv_std * (
        d_hat
        - jnp.mean(d_hat, axis=-1, keepdims=True)
        - x_hat * jnp.mean(d_hat * x_hat, axis=-1, keepdims=True)
    )
    g_x_share = lax.dynamic_slice_in_dim(g_x_full, col_start, share_cols, 1)
    g_gain = lax.dynamic_slice_in_dim(jnp.sum(g_hidden * x_hat, axis=0), col_start, share_cols, 0)
    g_bias = lax.dynamic_slice_in_dim(jnp.sum(g_hidden, axis=0), col_start, share_cols, 0)
    g_inputs = grad_share + g_x_share
    qkv_three = g_w_qkv.reshape(model_width, 3, att_width)
    summed = (
        lax.psum_scatter(qkv_three, "wide", scatter_dimension=0, tiled=True),
        lax.psum_scatter(g_w_out_rows, "wide", scatter_dimension=1, tiled=True),
        lax.psum_scatter(g_w_in, "wide", scatter_dimension=0, tiled=True),
        lax.psum_scatter(g_w_down, "wide", scatter_dimension=1, tiled=True),
    )
    g_qkv_part = lax.dynamic_slice_in_dim(summed[0], col_start, share_cols, 2)
    g_out_part = lax.dynamic_slice_in_dim(summed[1], col_start, share_cols, 0)
    small = lax.psum((g_gain, g_bias, g_b_in, g_b_down), "wide")
    return (
        mixed,
        g_inputs,
        small[0],
        small[1],
        g_qkv_part,
        g_out_part,
        summed[2],
        small[2],
        summed[3],
        small[3],
    )


def solution(mesh):
    placed = (
        P("wide", "narrow"),
        P("wide", "narrow"),
        P("wide"),
        P(),
        P(),
        P(),
        P(),
        P(None, "narrow"),
        P("narrow"),
        P("narrow", None),
        P("narrow"),
    )
    return jax.shard_map(
        on_device,
        mesh=mesh,
        in_specs=placed,
        out_specs=(
            P("wide", "narrow"),
            P("wide", "narrow"),
            P("narrow"),
            P("narrow"),
            P("wide", None, "narrow"),
            P("narrow", "wide"),
            P("wide", "narrow"),
            P("narrow"),
            P("narrow", "wide"),
            P("narrow"),
        ),
        check_vma=False,
    )
```

profile of v0, /device:TPU:0, one launch (start us, length us, event | category | flops | bytes accessed | tf_op | source)
XLA Modules:
  0.0 1303.8 jit_solution(5794400581022768838)
XLA Ops:
  9.4 24.3 %psum.42 = f32[]{:T(128)} all-reduce(f32[]{:T(128)} %bitcast.42), channel_id=1, replica_groups=mesh['wide'=8,'narrow'=4] {'wide'}, use_global_device_ids=true, to_apply=%region_9.10 | all-reduce | flops 1 | bytes 8 | tf_op jit(solution)/shard_map/psum | solution.py:148
  35.4 12.0 all-gather.3.cloned.1.call-done
  53.4 20.1 %fusion.57 = f32[2048,3072]{0,1:T(8,128)} fusion(bf16[1024,3072]{1,0:T(8,128)(2,1)} %param.32, f32[1024]{0:T(1024)S(1)} %copy-done.40, f32[1024]{0:T(1024)S(1)} %copy-done.42, f32[2048]{0:T(1024)S(1)} %add_rsqrt_fusion, f32[2048]{0:T(1024)S(1)} %broadcast_multiply_fusion.3, bf16[2048,1024]{1,0:T(8,128)(2,1)S(1)} %copy-done.16), kind=kOutput, calls=%fused_computation.161 | convolution fusion | flops 12897484800 | bytes 35676160 | tf_op jit(solution)/shard_map/dot_general | solution.py:166
  73.5 32.4 %reshape.583 = f32[2,1024,3,16,64]{1,0,4,3,2:T(2,128)} reshape(f32[2048,3072]{0,1:T(8,128)} %fusion.57) | data formatting | bytes 50331648 | tf_op jit(solution)/shard_map/reshape | solution.py:167
  106.0 8.9 slice.304
  114.8 21.4 %slice_bitcast_fusion = (f32[2,1024,16,64]{1,0,3,2:T(2,128)S(1)}, f32[2,1024,16,64]{1,0,3,2:T(2,128)S(1)}) fusion(f32[2,1024,3,16,64]{1,0,4,3,2:T(2,128)} %reshape.583), kind=kLoop, calls=%fused_computation.92 | loop fusion | bytes 33554432 | tf_op jit(solution)/shard_map/squeeze | solution.py:175
  156.1 14.5 %convert_reduce_fusion.1 = (f32[1024]{0:T(1024)}, bf16[2048,1024]{1,0:T(8,128)(2,1)S(1)}) fusion(bf16[1024,1024]{1,0:T(8,128)(2,1)S(1)} %copy-done, bf16[2048,1024]{1,0:T(8,128)(2,1)} %all-gather.5.cloned.1.call-done, f32[2048]{0:T(1024)S(1)} %bitcast.281, f32[2048,1024]{1,0:T(8,128)} %fusion.56, f32[1024]{0:T(1024)S(1)} %copy-done.37), kind=kOutput, calls=%fused_computation.95 | convolution fusion | flops 4357880832 | bytes 18890752 | tf_op jit(solution)/shard_map/dot_general | solution.py:203
  196.6 9.7 pad_maximum_fusion.2
  215.5 9.6 pad_maximum_fusion.3
  230.7 178.8 %while.35 = (s32[]{:T(128)}, bf16[2,1024,1024]{2,1,0:T(8,128)(2,1)}, f32[2,16,1024]{2,1,0:T(8,128)}, bf16[2,1024,1024]{1,2,0:T(8,128)(2,1)}, s32[2]{0:T(128)S(1)...) while((s32[]{:T(128)}, ...), condition=%wide.region_7.8_spmd, body=%wide.region_2.7_spmd.sunk | while | flops 3377989632 | bytes 247078176 | solution.py:188
  249.7 9.3 fusion.154
  259.1 8.5 fusion.155
  267.6 14.0 %fusion.149 = (f32[16,512]{1,0:T(8,128)S(1)}, f32[16,512,1024]{2,1,0:T(8,128)}) fusion(pred[512,1024]{1,0:T(8,128)(4,1)S(1)} %copy-done.13, bf16[512,16,64]{0,2,1:T(8,128)(2,1)S(1)} %bitcast.256, bf16[1024,16,64]{0,2,1:T(8,128)(2,1)S(1)} %bitcast.246), kind=kOutput, calls=%fused_computation.3.clone.1 | convolution fusion | flops 1098899456 | bytes 37257216 | tf_op jit(solution)/shard_map/while/body/eval_jaxpr/qhd,khd->hqk/dot_general | solution.py:54
  281.6 15.0 %fusion.150 = f32[16,512]{1,0:T(8,128)S(1)} fusion(f32[16,512,1024]{2,1,0:T(8,128)} %get-tuple-element.521, f32[16,512]{1,0:T(8,128)S(1)} %get-tuple-element.522, pred[512,1024]{1,0:T(8,128)(4,1)S(1)} %copy-done.13), kind=kLoop, calls=%fused_computation.4.clone.1 | loop fusion | flops 33546240 | bytes 34144256 | tf_op jit(solution)/shard_map/while/body/eval_jaxpr/reduce_sum | solution.py:78
  296.7 14.4 %fusion.151 = bf16[512,16,64]{0,2,1:T(8,128)(2,1)S(1)} fusion(bf16[1024,16,64]{0,2,1:T(8,128)(2,1)S(1)} %bitcast.263, f32[16,512,1024]{2,1,0:T(8,128)} %get-tuple-element.521, f32[16,512]{1,0:T(8,128)S(1)} %fusion.150, f32[16,512]{1,0:T(8,128)S(1)} %get-tuple-element.522, pred[512,1024]{1,0:T(8,128)(4,1)S(1)} %copy-done.13), kind=kOutput, calls=%fused_computation.16.clone.1 | convolution fusion | flops 1115684864 | bytes 37289984 | tf_op jit(solution)/shard_map/while/body/eval_jaxpr/hqk,khd->qhd/dot_general | solution.py:81
  338.8 9.2 fusion.154
  356.6 14.0 %fusion.149 = (f32[16,512]{1,0:T(8,128)S(1)}, f32[16,512,1024]{2,1,0:T(8,128)}) fusion(pred[512,1024]{1,0:T(8,128)(4,1)S(1)} %copy-done.13, bf16[512,16,64]{0,2,1:T(8,128)(2,1)S(1)} %bitcast.256, bf16[1024,16,64]{0,2,1:T(8,128)(2,1)S(1)} %bitcast.246), kind=kOutput, calls=%fused_computation.3.clone.1 | convolution fusion | flops 1098899456 | bytes 37257216 | tf_op jit(solution)/shard_map/while/body/eval_jaxpr/qhd,khd->hqk/dot_general | solution.py:54
  370.5 15.0 %fusion.150 = f32[16,512]{1,0:T(8,128)S(1)} fusion(f32[16,512,1024]{2,1,0:T(8,128)} %get-tuple-element.521, f32[16,512]{1,0:T(8,128)S(1)} %get-tuple-element.522, pred[512,1024]{1,0:T(8,128)(4,1)S(1)} %copy-done.13), kind=kLoop, calls=%fused_computation.4.clone.1 | loop fusion | flops 33546240 | bytes 34144256 | tf_op jit(solution)/shard_map/while/body/eval_jaxpr/reduce_sum | solution.py:78
  385.6 14.4 %fusion.151 = bf16[512,16,64]{0,2,1:T(8,128)(2,1)S(1)} fusion(bf16[1024,16,64]{0,2,1:T(8,128)(2,1)S(1)} %bitcast.263, f32[16,512,1024]{2,1,0:T(8,128)} %get-tuple-element.521, f32[16,512]{1,0:T(8,128)S(1)} %fusion.150, f32[16,512]{1,0:T(8,128)S(1)} %get-tuple-element.522, pred[512,1024]{1,0:T(8,128)(4,1)S(1)} %copy-done.13), kind=kOutput, calls=%fused_computation.16.clone.1 | convolution fusion | flops 1115684864 | bytes 37289984 | tf_op jit(solution)/shard_map/while/body/eval_jaxpr/hqk,khd->qhd/dot_general | solution.py:81
  409.5 10.1 fusion.53
  419.7 11.1 convolution_convert_fusion.2
  431.3 9.5 convolution_convert_fusion.1
  440.9 385.4 %while.36 = (s32[]{:T(128)}, f32[2,1024,16,64]{1,3,2,0:T(8,128)}, f32[2,1024,16,64]{1,3,2,0:T(8,128)}, bf16[2,1024,16,64]{1,3,2,0:T(8,128)(2,1)}, bf16[2,1024,10...) while((s32[]{:T(128)}, f32[2,1024,16,64]{1,3,2,0:T(8,128)}, ...), condition=%wide.region_13.14_spmd, body=%wide.region_10.13_spmd.sunk | while | flops 8223967232 | bytes 591404544 | solution.py:217
  476.3 12.2 multiply_reduce_fusion.7
  488.4 15.5 %multiply_convert_fusion.15 = bf16[16,512,512]{1,2,0:T(8,128)(2,1)} fusion(f32[16,512,512]{1,2,0:T(8,128)} %get-tuple-element.548, f32[16,512,512]{1,2,0:T(8,128)} %fusion.180, f32[16,512]{1,0:T(8,128)S(1)} %get-tuple-element.549), kind=kLoop, calls=%fused_computation.41.clone.1 | loop fusion | flops 12582912 | bytes 41975808 | tf_op jit(solution)/shard_map/while/body/eval_jaxpr/convert_element_type | solution.py:112
  523.6 13.7 %fusion.177 = f32[16,512,1024]{2,1,0:T(8,128)} fusion(bf16[512,16,64]{0,2,1:T(8,128)(2,1)S(1)} %bitcast.247, bf16[1024,16,64]{0,2,1:T(8,128)(2,1)S(1)} %bitcast.244), kind=kOutput, calls=%fused_computation.166.clone.1 | convolution fusion | flops 1073741824 | bytes 36700160 | tf_op jit(solution)/shard_map/while/body/eval_jaxpr/qhd,khd->hqk/dot_general | solution.py:54
  537.3 17.6 %bitcast_dynamic-update-slice_fusion.5 = bf16[2,1024,16,64]{1,3,2,0:T(8,128)(2,1)} fusion(bf16[2,1024,16,64]{1,3,2,0:T(8,128)(2,1)} %get-tuple-element.596, s32[]{:T(128)S(6)} %copy.108, f32[512,16,64]{0,2,1:T(8,128)} %fusion.183, bf16[512,16,64]{0,2,1:T(8,128)(2,1)} %bitcast.258, f32[16,512,1024]{2,1,0:T(8,128)} %fusion.177, ...), kind=kOutput, calls=%fused_computation.50.clone.1 | convolution fusion | flops 1108344832 | bytes 41451524 | tf_op jit(solution)/shard_map/while/body/eval_jaxpr/hqk,qhd->khd/dot_general | solution.py:129
  554.9 26.0 %multiply_reduce_fusion.6 = (f32[16,512]{1,0:T(8,128)S(1)}, f32[16,512,1024]{2,1,0:T(8,128)}) fusion(f32[16,512,1024]{2,1,0:T(8,128)} %fusion.177, f32[16,512]{1,0:T(8,128)S(1)} %get-tuple-element.539, pred[512,1024]{1,0:T(8,128)(4,1)} %fusion.179, bf16[512,16,64]{0,2,1:T(8,128)(2,1)} %bitcast.259, bf16[1024,16,64]{0,2,1:T(8,128)(2,1)} %bitcast.251), kind=kOutput, calls=%fused_computation.38.clone.1 | convolution fusion | flops 1115676672 | bytes 70844416 | tf_op jit(solution)/shard_map/while/body/eval_jaxpr/qhd,khd->hqk/dot_general | solution.py:108
  580.9 28.0 %multiply_convert_fusion.14 = bf16[16,512,1024]{2,1,0:T(8,128)(2,1)} fusion(f32[16,512,1024]{2,1,0:T(8,128)} %get-tuple-element.542, f32[16,512,1024]{2,1,0:T(8,128)} %fusion.177, f32[16,512]{1,0:T(8,128)S(1)} %get-tuple-element.543, f32[16,512]{1,0:T(8,128)S(1)} %get-tuple-element.539, pred[512,1024]{1,0:T(8,128)(4,1)} %fusion.179), kind=kLoop, calls=%fused_computation.37.clone.1 | loop fusion | flops 50331648 | bytes 84475904 | tf_op jit(solution)/shard_map/while/body/eval_jaxpr/convert_element_type | solution.py:112
  608.8 12.3 multiply_bitcast_fusion.6
  621.1 11.5 bitcast_dynamic-update-slice_fusion.4
  660.9 12.0 multiply_reduce_fusion.7
  672.9 15.3 %multiply_convert_fusion.15 = bf16[16,512,512]{1,2,0:T(8,128)(2,1)} fusion(f32[16,512,512]{1,2,0:T(8,128)} %get-tuple-element.548, f32[16,512,512]{1,2,0:T(8,128)} %fusion.180, f32[16,512]{1,0:T(8,128)S(1)} %get-tuple-element.549), kind=kLoop, calls=%fused_computation.41.clone.1 | loop fusion | flops 12582912 | bytes 41975808 | tf_op jit(solution)/shard_map/while/body/eval_jaxpr/convert_element_type | solution.py:112
  707.1 13.1 %fusion.177 = f32[16,512,1024]{2,1,0:T(8,128)} fusion(bf16[512,16,64]{0,2,1:T(8,128)(2,1)S(1)} %bitcast.247, bf16[1024,16,64]{0,2,1:T(8,128)(2,1)S(1)} %bitcast.244), kind=kOutput, calls=%fused_computation.166.clone.1 | convolution fusion | flops 1073741824 | bytes 36700160 | tf_op jit(solution)/shard_map/while/body/eval_jaxpr/qhd,khd->hqk/dot_general | solution.py:54
  720.2 17.4 %bitcast_dynamic-update-slice_fusion.5 = bf16[2,1024,16,64]{1,3,2,0:T(8,128)(2,1)} fusion(bf16[2,1024,16,64]{1,3,2,0:T(8,128)(2,1)} %get-tuple-element.596, s32[]{:T(128)S(6)} %copy.108, f32[512,16,64]{0,2,1:T(8,128)} %fusion.183, bf16[512,16,64]{0,2,1:T(8,128)(2,1)} %bitcast.258, f32[16,512,1024]{2,1,0:T(8,128)} %fusion.177, ...), kind=kOutput, calls=%fused_computation.50.clone.1 | convolution fusion | flops 1108344832 | bytes 41451524 | tf_op jit(solution)/shard_map/while/body/eval_jaxpr/hqk,qhd->khd/dot_general | solution.py:129
  737.6 26.0 %multiply_reduce_fusion.6 = (f32[16,512]{1,0:T(8,128)S(1)}, f32[16,512,1024]{2,1,0:T(8,128)}) fusion(f32[16,512,1024]{2,1,0:T(8,128)} %fusion.177, f32[16,512]{1,0:T(8,128)S(1)} %get-tuple-element.539, pred[512,1024]{1,0:T(8,128)(4,1)} %fusion.179, bf16[512,16,64]{0,2,1:T(8,128)(2,1)} %bitcast.259, bf16[1024,16,64]{0,2,1:T(8,128)(2,1)} %bitcast.251), kind=kOutput, calls=%fused_computation.38.clone.1 | convolution fusion | flops 1115676672 | bytes 70844416 | tf_op jit(solution)/shard_map/while/body/eval_jaxpr/qhd,khd->hqk/dot_general | solution.py:108
  763.6 28.0 %multiply_convert_fusion.14 = bf16[16,512,1024]{2,1,0:T(8,128)(2,1)} fusion(f32[16,512,1024]{2,1,0:T(8,128)} %get-tuple-element.542, f32[16,512,1024]{2,1,0:T(8,128)} %fusion.177, f32[16,512]{1,0:T(8,128)S(1)} %get-tuple-element.543, f32[16,512]{1,0:T(8,128)S(1)} %get-tuple-element.539, pred[512,1024]{1,0:T(8,128)(4,1)} %fusion.179), kind=kLoop, calls=%fused_computation.37.clone.1 | loop fusion | flops 50331648 | bytes 84475904 | tf_op jit(solution)/shard_map/while/body/eval_jaxpr/convert_element_type | solution.py:112
  791.5 12.3 multiply_bitcast_fusion.6
  803.8 11.6 bitcast_dynamic-update-slice_fusion.4
  845.9 30.1 %copy.57 = bf16[2,1024,3,16,64]{1,0,4,3,2:T(2,128)(2,1)S(1)} copy(bf16[2,1024,3,16,64]{1,4,3,0,2:T(8,128)(2,1)S(1)} %pad_maximum_fusion.1) | data formatting | bytes 25165824 | tf_op jit(solution)/shard_map/stack | solution.py:224
  883.3 21.0 %fusion.40 = f32[1024,3,1024]{2,0,1:T(8,128)} fusion(bf16[3,1024,2048]{2,1,0:T(8,128)(2,1)} %bitcast.274, f32[1024]{0:T(1024)S(1)} %copy-done.41, f32[1024]{0:T(1024)S(1)} %copy-done.43, f32[2048]{0:T(1024)S(1)} %copy-done.33, f32[2048]{0:T(1024)S(1)} %copy-done.28, bf16[2048,1024]{1,0:T(8,128)(2,1)} %all-gather.3.cloned.1.call-done), kind=kOutput, calls=%fused_computation.110 | convolution fusion | flops 12897484800 | bytes 29384704 | tf_op jit(solution)/shard_map/rd,rc->dc/dot_general | solution.py:228
  905.0 13.2 %fusion.52 = f32[1024,1024]{1,0:T(8,128)} fusion(bf16[2048,1024]{1,0:T(8,128)(2,1)} %all-gather.5.cloned.1.call-done, f32[2048]{0:T(1024)S(1)} %bitcast.284, f32[2048,1024]{1,0:T(8,128)} %fusion.56, f32[1024]{0:T(1024)S(1)} %copy-done.39), kind=kOutput, calls=%fused_computation.156 | convolution fusion | flops 4322230272 | bytes 16789504 | tf_op jit(solution)/shard_map/rf,rd->fd/dot_general | solution.py:202
  918.4 10.4 fusion.55
  928.9 26.1 %fusion.58 = (f32[1024]{0:T(1024)S(1)}, f32[1024]{0:T(1024)S(1)}, f32[2048]{0:T(1024)S(1)}, f32[2048]{0:T(1024)S(1)}, f32[2048,1024]{1,0:T(8,128)}, /*index=5*/f32[2048,1024]{1,0:T(8,128)}) fusion(f32[2048]{0:T(1024)S(1)} %copy-done.33, f32[2048]{0:T(1024)S(1)} %copy-done.28, bf16[2048,1024]{1,0:T(8,128)(2,1)} %all-gather.3.cloned.1.call-done, ...), kind=kOutput, calls=%fused_computation.162 | convolution fusion | flops 12910061568 | bytes 44085248 | tf_op jit(solution)/shard_map/dot_general | solution.py:229
  960.4 22.6 %all-reduce.2 = (f32[256]{0:T(256)}, f32[256]{0:T(256)}, f32[1024]{0:T(1024)}, f32[256]{0:T(256)}) all-reduce(f32[256]{0:T(256)S(1)} %dynamic_slice.77, f32[256]{0:T(256)S(1)} %dynamic_slice.78, f32[1024]{0:T(1024)S(1)} %copy-done.34, f32[256]{0:T(256)S(1)} %get-tuple-element.389), channel_id=1, replica_groups=mesh['wide'=8,'narrow'=4] {'wide'}, use_global_device_ids=true, to_apply=%region_18.19 | all-reduce | flops 1792 | bytes 14336 | tf_op jit(solution)/shard_map/psum | solution.py:252
  990.0 122.7 %reduce-scatter.8.cloned.1.call-done = f32[128,3,1024]{2,0,1:T(8,128)} async-done(((f32[1024,3,1024]{2,0,1:T(8,128)}), f32[128,3,1024]{2,0,1:T(8,128)}) %reduce-scatter.8.cloned.1.call-update) | async-done | bytes 1572880 | tf_op jit(solution)/shard_map/reduce_scatter | solution.py:245
  1114.5 90.3 %reduce-scatter.14.cloned.1.call-done = f32[1024,128]{1,0:T(8,128)} async-done(((f32[1024,1024]{1,0:T(8,128)}), f32[1024,128]{1,0:T(8,128)}) %reduce-scatter.14.cloned.1.call-update) | async-done | bytes 524304 | tf_op jit(solution)/shard_map/reduce_scatter | solution.py:248
  1204.8 92.0 %reduce-scatter.12.cloned.1.call-done = f32[128,1024]{1,0:T(8,128)} async-done(((f32[1024,1024]{1,0:T(8,128)}), f32[128,1024]{1,0:T(8,128)}) %reduce-scatter.12.cloned.1.call-update) | async-done | bytes 524304 | tf_op jit(solution)/shard_map/reduce_scatter | solution.py:247
  (264 shorter events, 270.6 us)
Async XLA Ops:
  7.2 148.9 %copy-start = (bf16[1024,1024]{1,0:T(8,128)(2,1)S(1)}, bf16[1024,1024]{1,0:T(8,128)(2,1)}, u32[]{:S(2)}) copy-start(bf16[1024,1024]{1,0:T(8,128)(2,1)} %param.36) | copy-start | bytes 6291460
  7.2 46.2 %copy-start.42 = (f32[1024]{0:T(1024)S(1)}, f32[1024]{0:T(1024)}, u32[]{:S(2)}) copy-start(f32[1024]{0:T(1024)} %param.30) | copy-start | bytes 12292
  7.2 46.2 %copy-start.40 = (f32[1024]{0:T(1024)S(1)}, f32[1024]{0:T(1024)}, u32[]{:S(2)}) copy-start(f32[1024]{0:T(1024)} %param.31) | copy-start | bytes 12292
  7.2 40.1 %all-gather.3.cloned.1.call-start = ((), (), s32[]{:S(2)}) async-start(), calls=%async_computation.5 | async-start | bytes 5242880 | tf_op jit(solution)/shard_map/all_gather | solution.py:151
  8.0 148.1 %all-gather.5.cloned.1.call-start = ((), (), s32[]{:S(2)}) async-start(), calls=%async_computation.7 | async-start | bytes 5242880 | tf_op jit(solution)/shard_map/all_gather | solution.py:152
  8.7 920.2 %all-reduce.5.cloned.1.call-start = ((), (), s32[]{:S(2)}) async-start(), calls=%async_computation.8 | async-start | bytes 8388608 | tf_op jit(solution)/shard_map/psum | solution.py:230
  34.4 121.6 %copy-start.29 = (f32[1,8,2,128]{3,1,2,0:T(8,128)}, f32[1,8,2,128]{3,1,2,0:T(8,128)S(1)}, u32[]{:S(2)}) copy-start(f32[1,8,2,128]{3,1,2,0:T(8,128)S(1)} %copy.82) | copy-start | bytes 24580
  35.4 154.5 %copy-start.24 = (f32[1024,16]{0,1:T(8,128)}, f32[1024,16]{0,1:T(8,128)S(1)}, u32[]{:S(2)}) copy-start(f32[1024,16]{0,1:T(8,128)S(1)} %get-tuple-element.397) | copy-start | bytes 196612
  50.3 98.9 %copy-start.27 = (f32[2048]{0:T(1024)}, f32[2048]{0:T(1024)S(1)}, u32[]{:S(2)}) copy-start(f32[2048]{0:T(1024)S(1)} %broadcast_multiply_fusion.3) | copy-start | bytes 24580
  53.4 95.8 %copy-start.32 = (f32[2048]{0:T(1024)}, f32[2048]{0:T(1024)S(1)}, u32[]{:S(2)}) copy-start(f32[2048]{0:T(1024)S(1)} %add_rsqrt_fusion) | copy-start | bytes 24580
  156.1 16.4 %copy-start.36 = (bf16[1024,1024]{1,0:T(8,128)(2,1)S(1)}, bf16[1024,1024]{1,0:T(8,128)(2,1)}, u32[]{:S(2)}) copy-start(bf16[1024,1024]{1,0:T(8,128)(2,1)} %param.34) | copy-start | bytes 6291460
  178.7 804.4 %reduce-scatter.10.cloned.1.call-start = ((), (), s32[]{:S(2)}) async-start(), calls=%async_computation.10 | async-start | bytes 4718592 | tf_op jit(solution)/shard_map/reduce_scatter | solution.py:246
  179.1 8.3 copy-start.19
  230.7 178.8 %copy-start.30 = (f32[1,8,2,128]{3,1,2,0:T(8,128)S(1)}, f32[1,8,2,128]{3,1,2,0:T(8,128)}, u32[]{:S(2)}) copy-start(f32[1,8,2,128]{3,1,2,0:T(8,128)} %copy-done.29) | copy-start | bytes 24580
  231.1 8.7 copy-start.9
  231.1 8.7 copy-start.10
  259.0 8.6 copy-start.4
  259.1 8.6 copy-start.13
  281.6 15.1 %copy-start.15 = (bf16[1,1024,1024]{1,2,0:T(8,128)(2,1)S(1)}, bf16[1,1024,1024]{1,2,0:T(8,128)(2,1)}, u32[]{:S(2)}) copy-start(bf16[1,1024,1024]{1,2,0:T(8,128)(2,1)} %get-tuple-element.518) | copy-start | bytes 6291460 | tf_op jit(solution)/shard_map/while
  320.4 8.6 copy-start.9
  320.4 8.6 copy-start.10
  348.0 8.6 copy-start.4
  348.0 8.6 copy-start.13
  370.5 15.1 %copy-start.15 = (bf16[1,1024,1024]{1,2,0:T(8,128)(2,1)S(1)}, bf16[1,1024,1024]{1,2,0:T(8,128)(2,1)}, u32[]{:S(2)}) copy-start(bf16[1,1024,1024]{1,2,0:T(8,128)(2,1)} %get-tuple-element.518) | copy-start | bytes 6291460 | tf_op jit(solution)/shard_map/while
  409.5 10.2 copy-start.38
  419.6 565.0 %reduce-scatter.6.cloned.1.call-start = ((), (), s32[]{:S(2)}) async-start(), calls=%async_computation.6 | async-start | bytes 5242880 | tf_op jit(solution)/shard_map/reduce_scatter | solution.py:190
  430.9 681.8 %reduce-scatter.8.cloned.1.call-start = ((), (), s32[]{:S(2)}) async-start(), calls=%async_computation.9 | async-start | bytes 14155776 | tf_op jit(solution)/shard_map/reduce_scatter | solution.py:245
  455.8 20.5 %copy-start.7 = (bf16[1,512,1024]{1,2,0:T(8,128)(2,1)}, bf16[1,512,1024]{1,2,0:T(8,128)(2,1)S(1)}, u32[]{:S(2)}) copy-start(bf16[1,512,1024]{1,2,0:T(8,128)(2,1)S(1)} %constant_dynamic-slice_fusion.29) | copy-start | bytes 3145732 | tf_op jit(solution)/shard_map/while
  460.6 7.6 copy-start.11
  463.8 12.5 copy-start.12
  488.4 18.7 %copy-start.2 = (f32[16,512,512]{1,2,0:T(8,128)S(1)}, f32[16,512,512]{1,2,0:T(8,128)}, u32[]{:S(2)}) copy-start(f32[16,512,512]{1,2,0:T(8,128)} %get-tuple-element.548) | copy-start | bytes 50331652 | tf_op jit(solution)/shard_map/while
  512.4 8.5 copy-start.3
  512.4 8.5 copy-start.8
  621.1 11.5 copy-start.6
  621.1 11.5 copy-start.14
  640.5 20.4 %copy-start.7 = (bf16[1,512,1024]{1,2,0:T(8,128)(2,1)}, bf16[1,512,1024]{1,2,0:T(8,128)(2,1)S(1)}, u32[]{:S(2)}) copy-start(bf16[1,512,1024]{1,2,0:T(8,128)(2,1)S(1)} %constant_dynamic-slice_fusion.29) | copy-start | bytes 3145732 | tf_op jit(solution)/shard_map/while
  648.4 12.5 copy-start.12
  672.9 18.4 %copy-start.2 = (f32[16,512,512]{1,2,0:T(8,128)S(1)}, f32[16,512,512]{1,2,0:T(8,128)}, u32[]{:S(2)}) copy-start(f32[16,512,512]{1,2,0:T(8,128)} %get-tuple-element.548) | copy-start | bytes 50331652 | tf_op jit(solution)/shard_map/while
  696.5 7.8 copy-start.3
  696.5 7.8 copy-start.8
  803.8 11.6 copy-start.6
  803.8 11.6 copy-start.14
  904.3 300.5 %reduce-scatter.14.cloned.1.call-start = ((), (), s32[]{:S(2)}) async-start(), calls=%async_computation.12 | async-start | bytes 4718592 | tf_op jit(solution)/shard_map/reduce_scatter | solution.py:248
  918.2 378.6 %reduce-scatter.12.cloned.1.call-start = ((), (), s32[]{:S(2)}) async-start(), calls=%async_computation.11 | async-start | bytes 4718592 | tf_op jit(solution)/shard_map/reduce_scatter | solution.py:247
  928.9 26.3 %copy-start.22 = (bf16[2048,256]{1,0:T(8,128)(2,1)S(1)}, bf16[2048,256]{1,0:T(8,128)(2,1)}, u32[]{:S(2)}) copy-start(bf16[2048,256]{1,0:T(8,128)(2,1)} %param.28) | copy-start | bytes 3145732
  928.9 31.5 %copy-start.34 = (f32[1024]{0:T(1024)S(1)}, f32[1024]{0:T(1024)}, u32[]{:S(2)}) copy-start(f32[1024]{0:T(1024)} %get-tuple-element.398) | copy-start | bytes 12292
  928.9 55.7 %copy-start.44 = (f32[256]{0:T(256)S(1)}, f32[256]{0:T(256)}, u32[]{:S(2)}) copy-start(f32[256]{0:T(256)} %param.37) | copy-start | bytes 3076
  955.2 341.6 %copy-start.1 = (bf16[1024,1024]{1,0:T(8,128)(2,1)S(1)}, bf16[1024,1024]{1,0:T(8,128)(2,1)}, u32[]{:S(2)}) copy-start(bf16[1024,1024]{1,0:T(8,128)(2,1)} %param.36) | copy-start | bytes 6291460
  (20 other events, 100.7 us)
Sparse Core Ops, SparseCore 0:
  9.6 37.7 all-gather.2
  48.9 35.0 all-gather.4
  178.8 85.3 all-reduce.4
  419.8 88.1 reduce-scatter.9
  510.3 44.2 reduce-scatter.5
  904.4 208.2 reduce-scatter.7
  1117.3 87.3 reduce-scatter.13
  1209.0 87.7 reduce-scatter.11
where the time goes:
time: 1310 us; the launch traced here: 1300 us
  matrix products  477 us (36%)
  waiting for transfers between devices  319 us (24%)
  local copies, waits for them, and re-layouts  228 us (17%)
  other arithmetic  197 us (15%)
  blocking collectives  46.9 us (4%)
  loops' own time  18.8 us (1%)
  between operations  16.2 us (1%)
    reduce_scatter x1, waiting for transfers between devices, on_device(): lax.psum_scatter(qkv_three, 'wide', scatter_dimension=0, tiled=True)  123 us
    dot_general x8, matrix products, block_scores(): jnp.einsum('qhd,khd->hqk', queries[first_row:last_row], key_rows[:last_ro...  93.8 us
    reduce_scatter x1, waiting for transfers between devices, on_device(): lax.psum_scatter(g_w_in, 'wide', scatter_dimension=0, tiled=True)  92 us
    reduce_scatter x1, waiting for transfers between devices, on_device(): lax.psum_scatter(g_w_down, 'wide', scatter_dimension=1, tiled=True)  90.3 us
    convert_element_type x4, other arithmetic, attend_backward(): grad_scores = (probs * (grad_probs - row_inner)).astype(jnp.bfloat16)  86.6 us
    dot_general x4, matrix products, attend_backward(): jnp.einsum('qhd,khd->hqk', grad_block, values[:last_row], preferred_eleme...  68.2 us
    reduce_sum x4, other arithmetic, attend_forward(): row_total = jnp.sum(exp_scores, axis=-1, keepdims=True)  48.6 us
    dot_general x4, matrix products, attend_forward(): jnp.einsum('hqk,khd->qhd', probs_low, values[:last_row], preferred_elemen...  45.9 us
  transfers between devices with their start and end apart: 8, of which 4 were waited for; matrix products, arithmetic and copies ran while one was open for 67% of the time, Pallas kernels for 0%

commit v1 on v0

--- a/solution.py
+++ b/solution.py
@@ -1,10 +1,23 @@
+import functools
+
 import jax
 import jax.numpy as jnp
+import numpy as np
 from jax import lax
+from jax.experimental import pallas as pl
+from jax.experimental.pallas import tpu as pltpu
 from jax.sharding import PartitionSpec as P
 
 HEAD_DIM = 64
 ROT = 32
+GELU_A = 0.7978845608028654
+GELU_B = 0.044715
+VMEM_BYTES = 56 * 1024 * 1024
+F32 = jnp.float32
+BF = jnp.bfloat16
+NN = (((1,), (0,)), ((), ()))
+NT = (((1,), (1,)), ((), ()))
+TN = (((0,), (0,)), ((), ()))
 
 
 norm_eps = 1e-05
@@ -264,6 +277,489 @@
     )
 
 
+LOG2E = 1.4426950408889634
+
+
+def mm(left, right, dims=NN):
+    return lax.dot_general(left, right, dims, preferred_element_type=F32)
+
+
+def norm_mlp_kernel(
+    place, scale, x0, x1, x2, x3, c0, c1, c2, c3, gain, bias, w_in, b_in, w_down,
+    hidden, grad_low, act, g_up, branch, g_hid, stats, sum_up, sum_grad,
+):
+    step = pl.program_id(0)
+    rows, cols = x0.shape
+    width, units = w_in.shape
+    own = place[0]
+    xs = [ref[...].astype(F32) for ref in (x0, x1, x2, x3)]
+    mean = jnp.sum(xs[0] + xs[1] + xs[2] + xs[3], axis=1, keepdims=True) * (1.0 / width)
+    cs = [x - mean for x in xs]
+    squares = cs[0] * cs[0] + cs[1] * cs[1] + cs[2] * cs[2] + cs[3] * cs[3]
+    inv_std = lax.rsqrt(jnp.sum(squares, axis=1, keepdims=True) * (1.0 / width) + norm_eps)
+    row = step * rows + lax.broadcasted_iota(jnp.int32, (rows, 1), 0)
+    weight = jnp.where(row < place[1], scale[0], 0.0)
+    for j, (centered, cot) in enumerate(zip(cs, (c0, c1, c2, c3))):
+        here = pl.ds(pl.multiple_of((own ^ j) * cols, cols), cols)
+        hidden[:, here] = (centered * inv_std * gain[:, here] + bias[:, here]).astype(BF)
+        low = (weight * cot[...].astype(F32)).astype(BF)
+        grad_low[:, here] = low
+        if j == 0:
+            sum_grad[...] = jnp.sum(low.astype(F32).reshape(rows // 8, 8, cols), axis=0)
+    lane = lax.broadcasted_iota(jnp.int32, (rows, 128), 1)
+    stats[...] = jnp.where(lane == 0, mean, inv_std)
+    h = hidden[...]
+    g = grad_low[...]
+    part = min(512, units)
+    for first in range(0, units, part):
+        here = pl.ds(first, part)
+        up = mm(h, w_in[:, here]) + b_in[:, here]
+        g_act = mm(g, w_down[here, :], NT)
+        square = up * up
+        tanh = jnp.tanh(up * (GELU_A + GELU_A * GELU_B * square))
+        half = 0.5 * up
+        plus = 1.0 + tanh
+        slope = 0.5 * plus + (half * (1.0 - tanh * tanh)) * (GELU_A + 3.0 * GELU_A * GELU_B * square)
+        g_here = (slope * g_act).astype(BF)
+        act[:, here] = (half * plus).astype(BF)
+        g_up[:, here] = g_here
+        sum_up[:, here] = jnp.sum(g_here.astype(F32).reshape(rows // 8, 8, part), axis=0)
+    branch[...] = mm(act[...], w_down[...]).astype(BF)
+    g_hid[...] = mm(g_up[...], w_in[...], NT).astype(BF)
+
+
+def norm_mlp(place, scale, xs, cots, gain, bias, w_in, b_in, w_down):
+    rows, cols = xs[0].shape
+    width, units = w_in.shape
+    tile = min(256, rows)
+    tiles = rows // tile
+
+    def rowed(size):
+        return pl.BlockSpec((tile, size), lambda i: (i, 0))
+
+    def whole(shape):
+        return pl.BlockSpec(shape, lambda i: (0, 0), pipeline_mode=pl.Buffered(1))
+
+    scalar = pl.BlockSpec(memory_space=pltpu.SMEM)
+    shape = jax.ShapeDtypeStruct
+    return pl.pallas_call(
+        norm_mlp_kernel,
+        grid=(tiles,),
+        in_specs=[scalar, scalar]
+        + [rowed(cols)] * 8
+        + [whole((1, width)), whole((1, width)), whole((width, units)), whole((1, units)), whole((units, width))],
+        out_specs=[rowed(width), rowed(width), rowed(units), rowed(units), rowed(width), rowed(width), rowed(128),
+                   pl.BlockSpec((8, units), lambda i: (i, 0)), pl.BlockSpec((8, cols), lambda i: (i, 0))],
+        out_shape=[shape((rows, width), BF), shape((rows, width), BF), shape((rows, units), BF), shape((rows, units), BF),
+                   shape((rows, width), BF), shape((rows, width), BF), shape((rows, 128), F32),
+                   shape((8 * tiles, units), F32), shape((8 * tiles, cols), F32)],
+        compiler_params=pltpu.CompilerParams(vmem_limit_bytes=VMEM_BYTES),
+        cost_estimate=pl.CostEstimate(flops=8 * rows * width * units, bytes_accessed=24 * rows * width, transcendentals=rows * units),
+        name="norm_mlp",
+    )(place, scale, *xs, *cots, gain, bias, w_in, b_in, w_down)
+
+
+def turn(field, cosine, sine):
+    lane = lax.broadcasted_iota(jnp.int32, field.shape, 1)
+    size = field.shape[1]
+    other = jnp.where(lane % 2 == 0, pltpu.roll(field, size - 1, 1), pltpu.roll(field, 1, 1))
+    return field * cosine + other * sine
+
+
+def attend_kernel(
+    place, hidden, grad_low, w_q, w_k, w_v, w_o, cosine, sine, cos_all, sin_all, branch_in, g_hid_in, gain, bias,
+    branch, g_hid, attended, g_qkv, sums,
+    k_aug, k_t, v_nat, v_t, q_nat, q_aug, d_out, att_s, gq_s, gk_acc, gv_acc, *, tiles, tile, pairs,
+):
+    step = pl.program_id(0)
+    own = place[0]
+    length = place[1]
+    rows = tiles * tile
+
+    @pl.when(step < tiles)
+    def project():
+        h = hidden[...]
+        cos = cosine[...]
+        sin = sine[...]
+        q_all = mm(h, w_q[...])
+        k_all = mm(h, w_k[...])
+        v_all = mm(h, w_v[...])
+        g_all = mm(grad_low[...], w_o[...], NT)
+        start = pl.multiple_of(step * tile, tile)
+        here = pl.ds(start, tile)
+        lane = lax.broadcasted_iota(jnp.int32, (tile, 128), 1)
+        key_row = start + lax.broadcasted_iota(jnp.int32, (tile, 128), 0)
+        closed = jnp.where(key_row < length, 0.0, -1e30)
+        first = lane < HEAD_DIM
+        sub = lax.broadcasted_iota(jnp.int32, (128, tile), 0)
+        for p in range(pairs):
+            cut = slice(128 * p, 128 * (p + 1))
+            q = turn(q_all[:, cut], cos, sin) * HEAD_DIM ** (-0.5)
+            k = turn(k_all[:, cut], cos, sin)
+            v = v_all[:, cut]
+            q_nat[p, here, :] = q.astype(BF)
+            v_nat[p, here, :] = v.astype(BF)
+            k_aug[2 * p, here, :] = jnp.where(first, k, jnp.where(lane == HEAD_DIM, closed, 0.0)).astype(BF)
+            k_aug[2 * p + 1, here, :] = jnp.where(first, jnp.where(lane == 0, closed, 0.0), k).astype(BF)
+            q_t = q.T
+            q_aug[2 * p, :, here] = jnp.where(sub < HEAD_DIM, q_t, jnp.where(sub == HEAD_DIM, 1.0, 0.0)).astype(BF)
+            q_aug[2 * p + 1, :, here] = jnp.where(sub < HEAD_DIM, jnp.where(sub == 0, 1.0, 0.0), q_t).astype(BF)
+            k_t[p, :, here] = k.T.astype(BF)
+            v_t[p, :, here] = v.T.astype(BF)
+            d_out[p, :, here] = g_all[:, cut].T
+
+    @pl.when((step >= tiles) & (step < tiles + pairs))
+    def attend():
+        p = step - tiles
+        lane = lax.broadcasted_iota(jnp.int32, (tile, 128), 1)
+        first = lane < HEAD_DIM
+        sub = lax.broadcasted_iota(jnp.int32, (128, tile), 0)
+        later = lax.broadcasted_iota(jnp.int32, (tile, tile), 0) > lax.broadcasted_iota(jnp.int32, (tile, tile), 1)
+        out_cut = pl.ds(pl.multiple_of(p * 128, 128), 128)
+        for i in range(tiles):
+            n = (i + 1) * tile
+            here = slice(i * tile, n)
+            outs = []
+            scaled = []
+            weights = []
+            row_inner = []
+            d_here = d_out[p, :, here]
+            for half in range(2):
+                s = mm(k_aug[2 * p + half, :n, :], q_aug[2 * p + half, :, here])
+                tail = jnp.where(later, -1e30, s[n - tile :])
+                s = tail if i == 0 else jnp.concatenate([s[: n - tile], tail], axis=0)
+                top = jnp.max(s, axis=0, keepdims=True)
+                e = jnp.exp(s - top)
+                share = 1.0 / jnp.sum(e, axis=0, keepdims=True)
+                e_low = e.astype(BF)
+                half_cut = slice(half * HEAD_DIM, (half + 1) * HEAD_DIM)
+                out = mm(v_t[p, half_cut, :n], e_low) * share
+                d = d_here[half_cut]
+                row_inner.append(jnp.sum(d * out, axis=0, keepdims=True) * share)
+                outs.append(out)
+                scaled.append(d * share)
+                weights.append((e, e_low))
+            att_s[here, out_cut] = jnp.concatenate(outs, axis=0).T.astype(BF)
+            d_scaled = jnp.concatenate(scaled, axis=0)
+            d_nat = d_scaled.T
+            q_here = q_nat[p, here, :]
+            g_q = []
+            for half in range(2):
+                e, e_low = weights[half]
+                mine_t = (sub < HEAD_DIM) if half == 0 else (sub >= HEAD_DIM)
+                mine = first if half == 0 else ~first
+                d_t = jnp.where(mine_t, d_scaled, 0.0).astype(BF)
+                g_s = (e * (mm(v_nat[p, :n, :], d_t) - row_inner[half])).astype(BF)
+                half_cut = slice(half * HEAD_DIM, (half + 1) * HEAD_DIM)
+                g_q.append(mm(k_t[p, half_cut, :n], g_s))
+                add_v = mm(e_low, jnp.where(mine, d_nat, 0.0).astype(BF))
+                add_k = mm(g_s, jnp.where(mine, q_here, 0.0).astype(BF))
+                if half == 0:
+                    first_v, first_k = add_v, add_k
+            add_v = first_v + add_v
+            add_k = first_k + add_k
+            if i < tiles - 1:
+                if i > 0:
+                    gv_acc[: n - tile] += add_v[: n - tile]
+                    gk_acc[: n - tile] += add_k[: n - tile]
+                gv_acc[here] = add_v[n - tile :]
+                gk_acc[here] = add_k[n - tile :]
+            else:
+                if i > 0:
+                    add_v = add_v + jnp.concatenate([gv_acc[: n - tile], jnp.zeros((tile, 128), F32)], axis=0)
+                    add_k = add_k + jnp.concatenate([gk_acc[: n - tile], jnp.zeros((tile, 128), F32)], axis=0)
+                gq_s[2, :, out_cut] = add_v.astype(BF)
+                gq_s[1, :, out_cut] = turn(add_k, cos_all[...], -sin_all[...]).astype(BF)
+            g_q = jnp.concatenate(g_q, axis=0).T * HEAD_DIM ** (-0.5)
+            gq_s[0, here, out_cut] = turn(g_q, cos_all[here, :], -sin_all[here, :]).astype(BF)
+
+    @pl.when(step >= tiles + pairs)
+    def finish():
+        start = pl.multiple_of((step - tiles - pairs) * tile, tile)
+        here = pl.ds(start, tile)
+        att = att_s[here, :]
+        attended[...] = att
+        total = mm(att, w_o[...]) + branch_in[...].astype(F32)
+        size = att.shape[1]
+        g_total = g_hid_in[...].astype(F32)
+        for j, w in enumerate((w_q, w_k, w_v)):
+            g = gq_s[j, here, :]
+            g_qkv[:, j * size : (j + 1) * size] = g
+            g_total += mm(g, w[...], NT)
+        width = total.shape[1]
+        share = width // 4
+        for j in range(4):
+            core_slot = (j & 1) ^ (own & 1)
+            y_slot = (j >> 1) ^ (own >> 1)
+            cut = slice(j * share, (j + 1) * share)
+            branch[core_slot, y_slot] = total[:, cut].astype(BF)
+            g_hid[core_slot, y_slot] = g_total[:, cut].astype(BF)
+        mean_part = jnp.sum(g_total * gain[...], axis=1, keepdims=True)
+        inner_part = jnp.sum(g_total * (hidden[...].astype(F32) - bias[...]), axis=1, keepdims=True)
+        lane = lax.broadcasted_iota(jnp.int32, (tile, 128), 1)
+        both = jnp.where(lane == 0, mean_part, inner_part)
+        sums[...] = both.T[:8, :]
+
+
+def attend(place, hidden, grad_low, w_qkv, w_out, cosine, sine, branch_in, g_hid_in, gain, bias):
+    rows, width = hidden.shape
+    share = width // 4
+    pairs = share // 128
+    tile = min(256, rows)
+    tiles = rows // tile
+    steps = 2 * tiles + pairs
+
+    def early(i, _):
+        return (jnp.minimum(i, tiles - 1), 0)
+
+    def late_row(i):
+        return jnp.maximum(i - tiles - pairs, 0)
+
+    def late(i, _):
+        return (late_row(i), 0)
+
+    def both(i, _):
+        return (jnp.where(i < tiles + pairs, jnp.minimum(i, tiles - 1), i - tiles - pairs), 0)
+
+    def whole(shape):
+        return pl.BlockSpec(shape, lambda i, _: (0, 0), pipeline_mode=pl.Buffered(1))
+
+    def column(j):
+        return pl.BlockSpec((width, share), lambda i, where: (0, 4 * j + where[0]), pipeline_mode=pl.Buffered(1))
+
+    shape = jax.ShapeDtypeStruct
+    slots = pl.BlockSpec((2, 2, tile, share), lambda i, _: (0, 0, late_row(i), 0))
+    return pl.pallas_call(
+        functools.partial(attend_kernel, tiles=tiles, tile=tile, pairs=pairs),
+        grid_spec=pltpu.PrefetchScalarGridSpec(
+            num_scalar_prefetch=1,
+            grid=(steps,),
+            in_specs=[
+                pl.BlockSpec((tile, width), both),
+                pl.BlockSpec((tile, width), early),
+                column(0), column(1), column(2),
+                pl.BlockSpec((share, width), lambda i, where: (where[0], 0), pipeline_mode=pl.Buffered(1)),
+                pl.BlockSpec((tile, 128), early),
+                pl.BlockSpec((tile, 128), early),
+                whole((rows, 128)), whole((rows, 128)),
+                pl.BlockSpec((tile, width), late),
+                pl.BlockSpec((tile, width), late),
+                whole((1, width)), whole((1, width)),
+            ],
+            out_specs=[
+                slots, slots,
+                pl.BlockSpec((tile, share), late),
+                pl.BlockSpec((tile, 3 * share), late),
+                pl.BlockSpec((8, tile), lambda i, _: (0, late_row(i))),
+            ],
+            scratch_shapes=[
+                pltpu.VMEM((2 * pairs, rows, 128), BF),
+                pltpu.VMEM((pairs, 128, rows), BF),
+                pltpu.VMEM((pairs, rows, 128), BF),
+                pltpu.VMEM((pairs, 128, rows), BF),
+                pltpu.VMEM((pairs, rows, 128), BF),
+                pltpu.VMEM((2 * pairs, 128, rows), BF),
+                pltpu.VMEM((pairs, 128, rows), F32),
+                pltpu.VMEM((rows, share), BF),
+                pltpu.VMEM((3, rows, share), BF),
+                pltpu.VMEM((rows, 128), F32),
+                pltpu.VMEM((rows, 128), F32),
+            ],
+        ),
+        out_shape=[
+            shape((2, 2, rows, share), BF), shape((2, 2, rows, share), BF),
+            shape((rows, share), BF), shape((rows, 3 * share), BF), shape((8, rows), F32),
+        ],
+        compiler_params=pltpu.CompilerParams(vmem_limit_bytes=VMEM_BYTES),
+        cost_estimate=pl.CostEstimate(flops=40 * rows * width * share, bytes_accessed=16 * rows * width, transcendentals=rows * rows * pairs),
+        name="attend",
+    )(place, hidden, grad_low, w_qkv, w_qkv, w_qkv, w_out, cosine, sine, cosine, sine, branch_in, g_hid_in, gain, bias)
+
+
+def weight_kernel(place, *refs):
+    out = refs[-1]
+    count = (len(refs) - 1) // 2
+    total = mm(refs[0][...], refs[count][...], TN)
+    for k in range(1, count):
+        total += mm(refs[k][...], refs[count + k][...], TN)
+    total = total.astype(BF)
+    mine = place[2]
+    out[mine, 0] = total[: total.shape[0] // 2]
+    out[1 - mine, 0] = total[total.shape[0] // 2 :]
+
+
+def weight_grad(place, lefts, rights):
+    rows, width = lefts[0].shape
+    units = rights[0].shape[1]
+    shards = 8
+    size = width // shards
+    column = pl.BlockSpec((rows, 2 * size), lambda i, _: (0, i))
+    whole = pl.BlockSpec((rows, units), lambda i, _: (0, 0), pipeline_mode=pl.Buffered(1))
+
+    def slot(i, where):
+        z = i ^ where[3]
+        return (0, 2 * (z & 1) + (z >> 1), 0, 0)
+
+    return pl.pallas_call(
+        weight_kernel,
+        grid_spec=pltpu.PrefetchScalarGridSpec(
+            num_scalar_prefetch=1,
+            grid=(shards // 2,),
+            in_specs=[column] * len(lefts) + [whole] * len(rights),
+            out_specs=pl.BlockSpec((2, 1, size, units), slot),
+        ),
+        out_shape=jax.ShapeDtypeStruct((2, shards // 2, size, units), BF),
+        compiler_params=pltpu.CompilerParams(vmem_limit_bytes=VMEM_BYTES),
+        cost_estimate=pl.CostEstimate(flops=2 * len(lefts) * rows * width * units, bytes_accessed=12 * rows * width, transcendentals=0),
+        name="weight_grad",
+    )(place, *lefts, *rights)
+
+
+def final_kernel(place, scale, keep_b, core_b, y_b, keep_g, core_g, y_g, x_ref, cot, stats, sums, gain, bias_down,
+                 mixed, g_x, col_gain, col_bias):
+    step = pl.program_id(0)
+    rows, cols = x_ref.shape
+    width = 4 * cols
+    x = x_ref[...].astype(F32)
+    branch = keep_b[0, 0].astype(F32) + core_b[0].astype(F32) + y_b[...].astype(F32)
+    mixed[...] = (x + (branch + bias_down[...])).astype(BF)
+    g = keep_g[0, 0].astype(F32) + core_g[0].astype(F32) + y_g[...].astype(F32)
+    mean = stats[:, 0:1]
+    inv_std = stats[:, 1:2]
+    x_hat = (x - mean) * inv_std
+    totals = jnp.concatenate([sums[...], jnp.zeros((120, rows), F32)], axis=0).T
+    row = step * rows + lax.broadcasted_iota(jnp.int32, (rows, 1), 0)
+    weight = jnp.where(row < place[1], scale[0], 0.0)
+    g_out = weight * cot[...].astype(F32)
+    inner = g * gain[...] - totals[:, 0:1] * (1.0 / width) - x_hat * (totals[:, 1:2] * (1.0 / width))
+    g_x[...] = g_out + inv_std * inner
+    col_gain[...] = jnp.sum((g * x_hat).reshape(rows // 8, 8, cols), axis=0)
+    col_bias[...] = jnp.sum(g.reshape(rows // 8, 8, cols), axis=0)
+
+
+def finish_rows(place, scale, keep_b, core_b, y_b, keep_g, core_g, y_g, x, cot, stats, sums, gain, bias_down):
+    rows, cols = x.shape
+    tile = min(256, rows)
+    tiles = rows // tile
+    rowed = pl.BlockSpec((tile, cols), lambda i: (i, 0))
+    kept = pl.BlockSpec((1, 1, tile, cols), lambda i: (0, 0, i, 0))
+    cored = pl.BlockSpec((1, tile, cols), lambda i: (0, i, 0))
+    flat = pl.BlockSpec((1, cols), lambda i: (0, 0))
+    eight = pl.BlockSpec((8, cols), lambda i: (i, 0))
+    scalar = pl.BlockSpec(memory_space=pltpu.SMEM)
+    shape = jax.ShapeDtypeStruct
+    return pl.pallas_call(
+        final_kernel,
+        grid=(tiles,),
+        in_specs=[scalar, scalar, kept, cored, rowed, kept, cored, rowed, rowed, rowed,
+                  pl.BlockSpec((tile, 128), lambda i: (i, 0)), pl.BlockSpec((8, tile), lambda i: (0, i)), flat, flat],
+        out_specs=[rowed, rowed, eight, eight],
+        out_shape=[shape((rows, cols), BF), shape((rows, cols), F32), shape((8 * tiles, cols), F32), shape((8 * tiles, cols), F32)],
+        compiler_params=pltpu.CompilerParams(vmem_limit_bytes=VMEM_BYTES),
+        cost_estimate=pl.CostEstimate(flops=20 * rows * cols, bytes_accessed=24 * rows * cols, transcendentals=0),
+        name="finish_rows",
+    )(place, scale, keep_b, core_b, y_b, keep_g, core_g, y_g, x, cot, stats, sums, gain, bias_down)
+
+
+def swap(value, axis, bit):
+    size = lax.axis_size(axis)
+    return lax.ppermute(value, axis, [(i, i ^ bit) for i in range(size)])
+
+
+def sum_small(value, axis):
+    bit = 1
+    while bit < lax.axis_size(axis):
+        value = value + swap(value, axis, bit)
+        bit *= 2
+    return value
+
+
+def scatter_wide(slots):
+    low = slots[0] + swap(slots[1], "wide", 1)
+    low = low[:2] + swap(low[2:], "wide", 2)
+    return low[0].astype(F32) + swap(low[1], "wide", 4).astype(F32)
+
+
+def on_device_fast(inputs, cotangent, lengths, ln_gain, ln_bias, w_qkv, w_out, w_in, b_in, w_down, b_down):
+    groups = lax.axis_size("wide")
+    column = lax.axis_index("narrow")
+    place_wide = lax.axis_index("wide")
+    rows_all, cols = inputs.shape
+    pad_len = rows_all // 2
+    width = w_qkv.shape[0]
+    units = w_in.shape[1]
+    count = 2.0 * jnp.sum(lengths.astype(F32))
+    scale = (groups * count / sum_small(count.reshape(1, 1), "wide")).reshape(1)
+    place = jnp.stack([column, lengths[0], place_wide & 1, place_wide >> 1]).astype(jnp.int32)
+    gain = ln_gain.reshape(1, width)
+    bias = ln_bias.reshape(1, width)
+    cosine, sine = turn_tables(pad_len)
+    fields = []
+    for s in range(2):
+        pieces = []
+        for whole in (inputs, cotangent):
+            own = whole[s * pad_len : (s + 1) * pad_len]
+            across = swap(own, "narrow", 2)
+            pieces.append((own, swap(own, "narrow", 1), across, swap(across, "narrow", 1)))
+        fields.append(pieces)
+    mlps = []
+    for s in range(2):
+        mlps.append(norm_mlp(place, scale, fields[s][0], fields[s][1], gain, bias, w_in, b_in.reshape(1, units), w_down))
+    hidden = [m[0] for m in mlps]
+    grad_low = [m[1] for m in mlps]
+    g_in_slots = weight_grad(place, hidden, [m[3] for m in mlps])
+    g_down_slots = weight_grad(place, grad_low, [m[2] for m in mlps])
+    atts = []
+    for s in range(2):
+        atts.append(attend(place, hidden[s], grad_low[s], w_qkv, w_out, cosine, sine, mlps[s][4], mlps[s][5], gain, bias))
+    g_qkv_slots = weight_grad(place, hidden, [a[3] for a in atts])
+    g_out_slots = weight_grad(place, grad_low, [a[2] for a in atts])
+    own_gain = lax.dynamic_slice_in_dim(ln_gain, column * cols, cols, 0).reshape(1, cols)
+    ends = []
+    for s in range(2):
+        branch, g_hid, _, _, sums = atts[s]
+        core_b = swap(branch[1], "narrow", 1)
+        core_g = swap(g_hid[1], "narrow", 1)
+        y_b = swap(branch[0, 1] + core_b[1], "narrow", 2)
+        y_g = swap(g_hid[0, 1] + core_g[1], "narrow", 2)
+        sums = sum_small(sums, "narrow")
+        ends.append(finish_rows(place, scale, branch, core_b, y_b, g_hid, core_g, y_g, fields[s][0][0], fields[s][1][0],
+                                mlps[s][6], sums, own_gain, b_down.reshape(1, cols)))
+    g_in = scatter_wide(g_in_slots)
+    g_down = scatter_wide(g_down_slots)
+    g_qkv = scatter_wide(g_qkv_slots)
+    g_out = scatter_wide(g_out_slots)
+    small = jnp.concatenate([
+        jnp.sum(ends[0][2] + ends[1][2], axis=0), jnp.sum(ends[0][3] + ends[1][3], axis=0),
+        jnp.sum(mlps[0][7] + mlps[1][7], axis=0), jnp.sum(mlps[0][8] + mlps[1][8], axis=0),
+    ])
+    small = sum_small(small, "wide")
+    return (
+        jnp.concatenate([ends[0][0], ends[1][0]], axis=0),
+        jnp.concatenate([ends[0][1], ends[1][1]], axis=0),
+        small[:cols],
+        small[cols : 2 * cols],
+        g_qkv.reshape(g_qkv.shape[0], 3, cols),
+        g_out.T,
+        g_in,
+        small[2 * cols : 2 * cols + units],
+        g_down.T,
+        small[2 * cols + units :],
+    )
+
+
+def turn_tables(length):
+    position = np.arange(length, dtype=np.float32)[:, None]
+    frequency = (10000.0 ** (-2.0 * np.arange(ROT // 2, dtype=np.float32) / ROT)).astype(np.float32)
+    angles = (position * frequency[None, :]).astype(np.float32)
+    cosine = np.ones((length, HEAD_DIM), np.float32)
+    sine = np.zeros((length, HEAD_DIM), np.float32)
+    cosine[:, :ROT] = np.repeat(np.cos(angles), 2, axis=1)
+    sine[:, 0:ROT:2] = -np.sin(angles)
+    sine[:, 1:ROT:2] = np.sin(angles)
+    return jnp.asarray(np.tile(cosine, (1, 2))), jnp.asarray(np.tile(sine, (1, 2)))
+
+
 def solution(mesh):
     placed = (
         P("wide", "narrow"),
@@ -278,8 +774,9 @@
         P("narrow", None),
         P("narrow"),
     )
+    paired = mesh.shape["narrow"] == 4 and mesh.shape["wide"] == 8
     return jax.shard_map(
-        on_device,
+        on_device_fast if paired else on_device,
         mesh=mesh,
         in_specs=placed,
         out_specs=(

time: 1310 us -> 321 us (0.25)
  matrix products: 477 us -> 0 us
  waiting for transfers between devices: 319 us -> 87.1 us
  local copies, waits for them, and re-layouts: 228 us -> 23 us
  other arithmetic: 197 us -> 17.7 us
  Pallas kernels: 0 us -> 137 us
  starting transfers between devices: 1.3 us -> 51.3 us
  blocking collectives: 46.9 us -> 0 us
  loops' own time: 18.8 us -> 0 us
    dot_general x40 -> x0, matrix products: 477 us -> none  [the longest x8 93.8 us: block_scores(): jnp.einsum('qhd,khd->hqk', queries[first_row:last_row], key_rows[:last_ro...]
    reduce_scatter x5 -> x0, waiting for transfers between devices: 305 us -> none  [the longest x1 123 us: on_device(): lax.psum_scatter(qkv_three, 'wide', scatter_dimension=0, tiled=True)]
    pallas_call x0 -> x10, Pallas kernels: none -> 137 us  [the longest x2 59.6 us: attend(): pl.pallas_call(functools.partial(attend_kernel, tiles=tiles, tile=tile, p...]
    ppermute x0 -> x42, waiting for transfers between devices: none -> 87.1 us  [swap(): return lax.ppermute(value, axis, [(i, i ^ bit) for i in range(size)])]
    convert_element_type x5 -> x0, other arithmetic: 86.7 us -> none  [the longest x4 86.6 us: attend_backward(): grad_scores = (probs * (grad_probs - row_inner)).astype(jnp.bfloat16)]
    reduce_sum x7 -> x3, other arithmetic: 59.7 us -> 0.99 us  [the longest x1 0.94 us: on_device_fast(): jnp.sum(ends[0][3] + ends[1][3], axis=0)]
    slice x25 -> x8, local copies, waits for them, and re-layouts: 59.8 us -> 5.13 us  [the longest x2 2.25 us: on_device_fast(): own = whole[s * pad_len:(s + 1) * pad_len]]
    ppermute x0 -> x42, starting transfers between devices: none -> 51.3 us  [swap(): return lax.ppermute(value, axis, [(i, i ^ bit) for i in range(size)])]
  transfers between devices with their start and end apart: 8 -> 42, of which waited for: 4 -> 18; matrix products, arithmetic and copies ran while one was open for 67% -> 12% of each run, Pallas kernels for 0% -> 43%
where the time goes in v1:
time: 321 us; the launch traced here: 320 us
  Pallas kernels  137 us (43%)
  waiting for transfers between devices  87.1 us (27%)
  starting transfers between devices  51.3 us (16%)
  local copies, waits for them, and re-layouts  23 us (7%)
  other arithmetic  17.7 us (6%)
  between operations  3.87 us (1%)
    ppermute x42, waiting for transfers between devices, swap(): return lax.ppermute(value, axis, [(i, i ^ bit) for i in range(size)])  87.1 us
    pallas_call x2, Pallas kernels, attend(): pl.pallas_call(functools.partial(attend_kernel, tiles=tiles, tile=tile, p...  59.6 us
    ppermute x42, starting transfers between devices, swap(): return lax.ppermute(value, axis, [(i, i ^ bit) for i in range(size)])  51.3 us
    pallas_call x2, Pallas kernels, norm_mlp(): pl.pallas_call(norm_mlp_kernel, grid=(tiles,), in_specs=[scalar, scalar]...  34.4 us
    pallas_call x4, Pallas kernels, weight_grad(): pl.pallas_call(weight_kernel, grid_spec=pltpu.PrefetchScalarGridSpec(num_...  33 us
    pallas_call x2, Pallas kernels, finish_rows(): pl.pallas_call(final_kernel, grid=(tiles,), in_specs=[scalar, scalar, kep...  9.52 us
    squeeze x4, local copies, waits for them, and re-layouts, scatter_wide(): low = slots[0] + swap(slots[1], 'wide', 1)  6.45 us
  transfers between devices with their start and end apart: 42, of which 18 were waited for; matrix products, arithmetic and copies ran while one was open for 12% of the time, Pallas kernels for 43%

profile of v1, /device:TPU:0, one launch (start us, length us, event | category | flops | bytes accessed | tf_op | source)
XLA Modules:
  0.0 319.5 jit_solution(17901451526363404856)
XLA Ops:
  0.7 1.4 fusion.12
  2.0 3.0 collective-permute-start.4
  6.0 1.9 collective-permute-start.19
  8.6 2.9 collective-permute-start
  12.9 2.9 collective-permute-start.1
  17.2 4.0 %collective-permute-start.2 = (f32[1,1]{1,0:T(1,128)}, f32[1,1]{1,0:T(1,128)}, u32[]{:S(2)}, u32[]{:S(2)}) collective-permute-start(f32[1,1]{1,0:T(1,128)} %add.94), channel_id=1, source_target_pairs={{0,16},{4,20},{8,24},{12,28},{16,0},{20,4},{24,8},{28,12},{1,17},{... | collective-permute-start | bytes 20 | tf_op jit(solution)/shard_map/ppermute | solution.py:666
  21.9 7.1 %collective-permute-done.16.x2 = bf16[1024,256]{1,0:T(8,128)(2,1)S(1)} collective-permute-done((bf16[1024,256]{1,0:T(8,128)(2,1)S(1)}, bf16[1024,256]{1,0:T(8,128)(2,1)S(1)}, u32[]{:S(2)}, u32[]{:S(2)}) %collective-permute-start.16) | collective-permute-done | bytes 524320 | tf_op jit(solution)/shard_map/ppermute | solution.py:666
  29.1 11.2 %collective-permute-done.19.c2 = bf16[1024,256]{1,0:T(8,128)(2,1)S(1)} collective-permute-done((bf16[1024,256]{1,0:T(8,128)(2,1)S(1)}, bf16[1024,256]{1,0:T(8,128)(2,1)S(1)}, u32[]{:S(2)}, u32[]{:S(2)}) %collective-permute-start.19) | collective-permute-done | bytes 524320 | tf_op jit(solution)/shard_map/ppermute | solution.py:666
  43.5 7.3 %collective-permute-done.7.c2 = bf16[1024,256]{1,0:T(8,128)(2,1)} collective-permute-done((bf16[1024,256]{1,0:T(8,128)(2,1)}, bf16[1024,256]{1,0:T(8,128)(2,1)}, u32[]{:S(2)}, u32[]{:S(2)}) %collective-permute-start.7) | collective-permute-done | bytes 524320 | tf_op jit(solution)/shard_map/ppermute | solution.py:666
  51.4 17.1 %norm_mlp.3 = (bf16[1024,1024]{1,0:T(8,128)(2,1)}, bf16[1024,1024]{1,0:T(8,128)(2,1)}, bf16[1024,1024]{1,0:T(8,128)(2,1)}, bf16[1024,1024]{1,0:T(8,128)(2,1)}, b...) custom-call(s32[4]{0:T(128)} %pad_add_fusion.place, ...), custom_call_target="tpu_custom_call" | custom-call | flops 8589934592 | bytes 25165824 | tf_op jit(solution)/shard_map/norm_mlp/pallas_call | solution.py:345
  68.6 29.8 %attend.3 = (bf16[2,2,1024,256]{3,2,1,0:T(8,128)(2,1)}, bf16[2,2,1024,256]{3,2,1,0:T(8,128)(2,1)}, bf16[1024,256]{1,0:T(8,128)(2,1)}, bf16[1024,768]{1,0:T(8,128)(2,1)}, f32[8,1024]{1,0:T(8,128)}) custom-call(s32[4]{0:T(128)} %pad_add_fusion.place, bf16[1024,1024]{1,0:T(8,128)(2,1)} %get-tuple-element.55.hidden.refs_1_, ...), custom_call_target="tpu_custom_call" | custom-call | flops 10737418240 | bytes 16777216 | tf_op jit(solution)/shard_map/attend/pallas_call | solution.py:532
  99.0 2.3 slice_bitcast_fusion.5
  104.4 17.3 %norm_mlp.2 = (bf16[1024,1024]{1,0:T(8,128)(2,1)}, bf16[1024,1024]{1,0:T(8,128)(2,1)}, bf16[1024,1024]{1,0:T(8,128)(2,1)}, bf16[1024,1024]{1,0:T(8,128)(2,1)}, b...) custom-call(s32[4]{0:T(128)} %pad_add_fusion.place, ...), custom_call_target="tpu_custom_call" | custom-call | flops 8589934592 | bytes 25165824 | tf_op jit(solution)/shard_map/norm_mlp/pallas_call | solution.py:345
  121.8 9.4 %weight_grad.6 = bf16[2,4,128,1024]{3,2,1,0:T(8,128)(2,1)} custom-call(s32[4]{0:T(128)} %pad_add_fusion.place, bf16[1024,1024]{1,0:T(8,128)(2,1)} %get-tuple-element.46.hidden.refs_0_, bf16[1024,1024]{1,0:T(8,128)(2,1)} %get-tuple-element.55.hidden.refs_1_, bf16[1024,1024]{1,0:T(8,128)(2,1)} %get-tuple-element.78.refs_2_, ...), custom_call_target="tpu_custom_call" | custom-call | flops 4294967296 | bytes 12582912 | tf_op jit(solution)/shard_map/weight_grad/pallas_call | solution.py:603
  131.2 2.3 slice_bitcast_fusion.2
  133.4 9.4 %weight_grad.7 = bf16[2,4,128,1024]{3,2,1,0:T(8,128)(2,1)} custom-call(s32[4]{0:T(128)} %pad_add_fusion.place, bf16[1024,1024]{1,0:T(8,128)(2,1)} %get-tuple-element.47.grad_low.refs_0_, bf16[1024,1024]{1,0:T(8,128)(2,1)} %get-tuple-element.56.grad_low.refs_1_, bf16[1024,1024]{1,0:T(8,128)(2,1)} %get-tuple-element.80.refs_2_, ...), custom_call_target="tpu_custom_call" | custom-call | flops 4294967296 | bytes 12582912 | tf_op jit(solution)/shard_map/weight_grad/pallas_call | solution.py:603
  142.8 2.3 slice_bitcast_fusion
  145.1 29.9 %attend.2 = (bf16[2,2,1024,256]{3,2,1,0:T(8,128)(2,1)}, bf16[2,2,1024,256]{3,2,1,0:T(8,128)(2,1)}, bf16[1024,256]{1,0:T(8,128)(2,1)}, bf16[1024,768]{1,0:T(8,128)(2,1)}, f32[8,1024]{1,0:T(8,128)}) custom-call(s32[4]{0:T(128)} %pad_add_fusion.place, bf16[1024,1024]{1,0:T(8,128)(2,1)} %get-tuple-element.46.hidden.refs_0_, ...), custom_call_target="tpu_custom_call" | custom-call | flops 10737418240 | bytes 16777216 | tf_op jit(solution)/shard_map/attend/pallas_call | solution.py:532
  175.2 5.9 %weight_grad.5 = bf16[2,4,128,256]{3,2,1,0:T(8,128)(2,1)} custom-call(s32[4]{0:T(128)} %pad_add_fusion.place, bf16[1024,1024]{1,0:T(8,128)(2,1)} %get-tuple-element.47.grad_low.refs_0_, bf16[1024,1024]{1,0:T(8,128)(2,1)} %get-tuple-element.56.grad_low.refs_1_, bf16[1024,256]{1,0:T(8,128)(2,1)} %get-tuple-element.76.refs_2_, ...), custom_call_target="tpu_custom_call" | custom-call | flops 1073741824 | bytes 12582912 | tf_op jit(solution)/shard_map/weight_grad/pallas_call | solution.py:603
  182.2 1.8 collective-permute-start.33
  185.1 8.3 %weight_grad.4 = bf16[2,4,128,768]{3,2,1,0:T(8,128)(2,1)} custom-call(s32[4]{0:T(128)} %pad_add_fusion.place, bf16[1024,1024]{1,0:T(8,128)(2,1)} %get-tuple-element.46.hidden.refs_0_, bf16[1024,1024]{1,0:T(8,128)(2,1)} %get-tuple-element.55.hidden.refs_1_, bf16[1024,768]{1,0:T(8,128)(2,1)} %get-tuple-element.74.refs_2_, ...), custom_call_target="tpu_custom_call" | custom-call | flops 3221225472 | bytes 12582912 | tf_op jit(solution)/shard_map/weight_grad/pallas_call | solution.py:603
  194.5 1.6 collective-permute-start.34
  197.7 1.7 collective-permute-start.26
  200.0 1.7 collective-permute-start.14
  201.7 1.8 collective-permute-start.39
  203.9 2.7 collective-permute-start.35
  209.1 1.8 collective-permute-start.36
  211.7 6.3 %collective-permute-done.30 = bf16[4,128,768]{2,1,0:T(8,128)(2,1)} collective-permute-done((bf16[4,128,768]{2,1,0:T(8,128)(2,1)}, bf16[4,128,768]{2,1,0:T(8,128)(2,1)}, u32[]{:S(2)}, u32[]{:S(2)}) %collective-permute-start.30) | collective-permute-done | bytes 786464 | tf_op jit(solution)/shard_map/ppermute | solution.py:666
  218.0 1.5 fusion.2
  221.6 2.0 fusion.4
  223.7 16.8 %collective-permute-done.39 = bf16[4,128,1024]{2,1,0:T(8,128)(2,1)} collective-permute-done((bf16[4,128,1024]{2,1,0:T(8,128)(2,1)}, bf16[4,128,1024]{2,1,0:T(8,128)(2,1)}, u32[]{:S(2)}, u32[]{:S(2)}) %collective-permute-start.39) | collective-permute-done | bytes 1048608 | tf_op jit(solution)/shard_map/ppermute | solution.py:666
  240.4 1.7 collective-permute-start.24
  242.1 1.4 fusion
  243.5 18.1 %collective-permute-done.36 = bf16[4,128,1024]{2,1,0:T(8,128)(2,1)} collective-permute-done((bf16[4,128,1024]{2,1,0:T(8,128)(2,1)}, bf16[4,128,1024]{2,1,0:T(8,128)(2,1)}, u32[]{:S(2)}, u32[]{:S(2)}) %collective-permute-start.36) | collective-permute-done | bytes 1048608 | tf_op jit(solution)/shard_map/ppermute | solution.py:666
  261.6 1.7 collective-permute-start.22
  263.3 1.4 fusion.1
  269.0 2.7 collective-permute-start.32
  271.6 1.9 fusion.6
  273.5 8.5 %collective-permute-done.32 = bf16[128,768]{1,0:T(8,128)(2,1)S(1)} collective-permute-done((bf16[128,768]{1,0:T(8,128)(2,1)S(1)}, bf16[128,768]{1,0:T(8,128)(2,1)S(1)}, u32[]{:S(2)}, u32[]{:S(2)}) %collective-permute-start.32) | collective-permute-done | bytes 196640 | tf_op jit(solution)/shard_map/ppermute | solution.py:666
  283.5 3.8 %collective-permute-start.37 = (bf16[2,128,1024]{2,1,0:T(8,128)(2,1)}, bf16[2,128,1024]{2,1,0:T(8,128)(2,1)S(1)}, u32[]{:S(2)}, u32[]{:S(2)}) collective-permute-start(bf16[2,128,1024]{2,1,0:T(8,128)(2,1)} %slice.197), channel_id=1, source_target_pairs={{0,8},{4,12},{8,0},{12,4},{16,24},{20,28},{24,16},{28,20},{1,9},{5... | collective-permute-start | bytes 1572872 | tf_op jit(solution)/shard_map/ppermute | solution.py:666
  288.5 4.8 %finish_rows.3 = (bf16[1024,256]{1,0:T(8,128)(2,1)}, f32[1024,256]{1,0:T(8,128)}, f32[32,256]{1,0:T(8,128)}, f32[32,256]{1,0:T(8,128)}) custom-call(s32[4]{0:T(128)} %pad_add_fusion.place, f32[1]{0:T(128)} %bitcast.5.scale, bf16[2,2,1024,256]{3,2,1,0:T(8,128)(2,1)} %get-tuple-element.59.keep_b, bf16[2,1024,256]{2,1,0:T(8,128)(2,1)} %collective-permute-done.21.core_b, ...), custom_call_target="tpu_custom_call" | custom-call | flops 5242880 | bytes 6291456 | tf_op jit(solution)/shard_map/finish_rows/pallas_call | solution.py:651
  293.3 3.8 %collective-permute-done.10.y_b = bf16[1024,256]{1,0:T(8,128)(2,1)} collective-permute-done((bf16[1024,256]{1,0:T(8,128)(2,1)}, bf16[1024,256]{1,0:T(8,128)(2,1)}, u32[]{:S(2)}, u32[]{:S(2)}) %collective-permute-start.10) | collective-permute-done | bytes 524320 | tf_op jit(solution)/shard_map/ppermute | solution.py:666
  297.1 4.8 %finish_rows.2 = (bf16[1024,256]{1,0:T(8,128)(2,1)}, f32[1024,256]{1,0:T(8,128)}, f32[32,256]{1,0:T(8,128)}, f32[32,256]{1,0:T(8,128)}) custom-call(s32[4]{0:T(128)} %pad_add_fusion.place, f32[1]{0:T(128)} %bitcast.5.scale, bf16[2,2,1024,256]{3,2,1,0:T(8,128)(2,1)} %get-tuple-element.50.keep_b, bf16[2,1024,256]{2,1,0:T(8,128)(2,1)} %copy-done.5, ...), custom_call_target="tpu_custom_call" | custom-call | flops 5242880 | bytes 6291456 | tf_op jit(solution)/shard_map/finish_rows/pallas_call | solution.py:651
  303.6 2.5 collective-permute-start.38
  306.6 1.4 collective-permute-start.28
  308.0 1.5 pad_maximum_fusion
  310.3 2.6 collective-permute-start.29
  313.9 2.5 collective-permute-done.29
  (169 shorter events, 35.5 us)
Async XLA Ops:
  2.0 49.4 %copy-start.10 = (bf16[1024,256]{1,0:T(8,128)(2,1)}, bf16[1024,256]{1,0:T(8,128)(2,1)S(1)}, u32[]{:S(2)}) copy-start(bf16[1024,256]{1,0:T(8,128)(2,1)S(1)} %get-tuple-element.105.x0.x_ref) | copy-start | bytes 1572868
  2.0 66.5 %copy-start.9 = (bf16[1024,256]{1,0:T(8,128)(2,1)}, bf16[1024,256]{1,0:T(8,128)(2,1)S(1)}, u32[]{:S(2)}) copy-start(bf16[1024,256]{1,0:T(8,128)(2,1)S(1)} %get-tuple-element.104.x0.x_ref) | copy-start | bytes 1572868
  2.0 19.9 %collective-permute-start.4 = (bf16[1024,256]{1,0:T(8,128)(2,1)S(1)}, bf16[1024,256]{1,0:T(8,128)(2,1)}, u32[]{:S(2)}, u32[]{:S(2)}) collective-permute-start(bf16[1024,256]{1,0:T(8,128)(2,1)S(1)} %get-tuple-element.104.x0.x_ref), channel_id=1, source_target_pairs={{0,2},{1,3},{2,0},{3,1},{4,6},{5,7},{6,4},{7,5},{8,10},{9,11},{10,... | collective-permute-start | bytes 1572872 | tf_op jit(solution)/shard_map/ppermute | solution.py:666
  5.1 24.0 %collective-permute-start.16 = (bf16[1024,256]{1,0:T(8,128)(2,1)S(1)}, bf16[1024,256]{1,0:T(8,128)(2,1)S(1)}, u32[]{:S(2)}, u32[]{:S(2)}) collective-permute-start(bf16[1024,256]{1,0:T(8,128)(2,1)S(1)} %get-tuple-element.105.x0.x_ref), channel_id=1, source_target_pairs={{0,2},{1,3},{2,0},{3,1},{4,6},{5,7},{6,4},{7,5},{8,10},{9,11},{10,... | collective-permute-start | bytes 1572872 | tf_op jit(solution)/shard_map/ppermute | solution.py:666
  6.0 45.4 %copy-start.11 = (bf16[1024,256]{1,0:T(8,128)(2,1)}, bf16[1024,256]{1,0:T(8,128)(2,1)S(1)}, u32[]{:S(2)}) copy-start(bf16[1024,256]{1,0:T(8,128)(2,1)S(1)} %get-tuple-element.103.c0.cot) | copy-start | bytes 1572868
  6.0 34.2 %collective-permute-start.19 = (bf16[1024,256]{1,0:T(8,128)(2,1)S(1)}, bf16[1024,256]{1,0:T(8,128)(2,1)S(1)}, u32[]{:S(2)}, u32[]{:S(2)}) collective-permute-start(bf16[1024,256]{1,0:T(8,128)(2,1)S(1)} %get-tuple-element.103.c0.cot), channel_id=1, source_target_pairs={{0,2},{1,3},{2,0},{3,1},{4,6},{5,7},{6,4},{7,5},{8,10},{9,11},{10,... | collective-permute-start | bytes 1572872 | tf_op jit(solution)/shard_map/ppermute | solution.py:666
  8.0 35.0 %collective-permute-start.15 = (bf16[1024,256]{1,0:T(8,128)(2,1)S(1)}, bf16[1024,256]{1,0:T(8,128)(2,1)S(1)}, u32[]{:S(2)}, u32[]{:S(2)}) collective-permute-start(bf16[1024,256]{1,0:T(8,128)(2,1)S(1)} %get-tuple-element.105.x0.x_ref), channel_id=1, source_target_pairs={{0,1},{1,0},{2,3},{3,2},{4,5},{5,4},{6,7},{7,6},{8,9},{9,8},{10,11... | collective-permute-start | bytes 1572872 | tf_op jit(solution)/shard_map/ppermute | solution.py:666
  8.6 3.6 %collective-permute-start = (f32[1,1]{1,0:T(1,128)}, f32[1,1]{1,0:T(1,128)}, u32[]{:S(2)}, u32[]{:S(2)}) collective-permute-start(f32[1,1]{1,0:T(1,128)} %bitcast.4), channel_id=1, source_target_pairs={{0,4},{4,0},{8,12},{12,8},{16,20},{20,16},{24,28},{28,24},{1,5},{5... | collective-permute-start | bytes 20 | tf_op jit(solution)/shard_map/ppermute | solution.py:666
  12.9 3.6 %collective-permute-start.1 = (f32[1,1]{1,0:T(1,128)}, f32[1,1]{1,0:T(1,128)}, u32[]{:S(2)}, u32[]{:S(2)}) collective-permute-start(f32[1,1]{1,0:T(1,128)} %add.93), channel_id=1, source_target_pairs={{0,8},{4,12},{8,0},{12,4},{16,24},{20,28},{24,16},{28,20},{1,9},{5... | collective-permute-start | bytes 20 | tf_op jit(solution)/shard_map/ppermute | solution.py:666
  17.2 4.6 %collective-permute-start.2 = (f32[1,1]{1,0:T(1,128)}, f32[1,1]{1,0:T(1,128)}, u32[]{:S(2)}, u32[]{:S(2)}) collective-permute-start(f32[1,1]{1,0:T(1,128)} %add.94), channel_id=1, source_target_pairs={{0,16},{4,20},{8,24},{12,28},{16,0},{20,4},{24,8},{28,12},{1,17},{... | collective-permute-start | bytes 20 | tf_op jit(solution)/shard_map/ppermute | solution.py:666
  21.8 29.0 %collective-permute-start.7 = (bf16[1024,256]{1,0:T(8,128)(2,1)}, bf16[1024,256]{1,0:T(8,128)(2,1)}, u32[]{:S(2)}, u32[]{:S(2)}) collective-permute-start(bf16[1024,256]{1,0:T(8,128)(2,1)} %get-tuple-element.102.c0.cot), channel_id=1, source_target_pairs={{0,2},{1,3},{2,0},{3,1},{4,6},{5,7},{6,4},{7,5},{8,10},{9,11},{10,... | collective-permute-start | bytes 1572872 | tf_op jit(solution)/shard_map/ppermute | solution.py:666
  21.9 28.9 %collective-permute-start.18 = (bf16[1024,256]{1,0:T(8,128)(2,1)S(1)}, bf16[1024,256]{1,0:T(8,128)(2,1)}, u32[]{:S(2)}, u32[]{:S(2)}) collective-permute-start(bf16[1024,256]{1,0:T(8,128)(2,1)S(1)} %get-tuple-element.103.c0.cot), channel_id=1, source_target_pairs={{0,1},{1,0},{2,3},{3,2},{4,5},{5,4},{6,7},{7,6},{8,9},{9,8},{10,11... | collective-permute-start | bytes 1572872 | tf_op jit(solution)/shard_map/ppermute | solution.py:666
  29.1 22.3 %collective-permute-start.17 = (bf16[1024,256]{1,0:T(8,128)(2,1)S(1)}, bf16[1024,256]{1,0:T(8,128)(2,1)}, u32[]{:S(2)}, u32[]{:S(2)}) collective-permute-start(bf16[1024,256]{1,0:T(8,128)(2,1)S(1)} %collective-permute-done.16.x2), channel_id=1, source_target_pairs={{0,1},{1,0},{2,3},{3,2},{4,5},{5,4},{6,7},{7,6},{8,9},{9,8},{10,11... | collective-permute-start | bytes 1572872 | tf_op jit(solution)/shard_map/ppermute | solution.py:666
  40.3 11.1 %collective-permute-start.20 = (bf16[1024,256]{1,0:T(8,128)(2,1)S(1)}, bf16[1024,256]{1,0:T(8,128)(2,1)}, u32[]{:S(2)}, u32[]{:S(2)}) collective-permute-start(bf16[1024,256]{1,0:T(8,128)(2,1)S(1)} %collective-permute-done.19.c2), channel_id=1, source_target_pairs={{0,1},{1,0},{2,3},{3,2},{4,5},{5,4},{6,7},{7,6},{8,9},{9,8},{10,11... | collective-permute-start | bytes 1572872 | tf_op jit(solution)/shard_map/ppermute | solution.py:666
  43.0 59.3 %collective-permute-start.3 = (bf16[1024,256]{1,0:T(8,128)(2,1)S(1)}, bf16[1024,256]{1,0:T(8,128)(2,1)S(1)}, u32[]{:S(2)}, u32[]{:S(2)}) collective-permute-start(bf16[1024,256]{1,0:T(8,128)(2,1)S(1)} %get-tuple-element.104.x0.x_ref), channel_id=1, source_target_pairs={{0,1},{1,0},{2,3},{3,2},{4,5},{5,4},{6,7},{7,6},{8,9},{9,8},{10,11... | collective-permute-start | bytes 1572872 | tf_op jit(solution)/shard_map/ppermute | solution.py:666
  50.8 51.7 %collective-permute-start.6 = (bf16[1024,256]{1,0:T(8,128)(2,1)}, bf16[1024,256]{1,0:T(8,128)(2,1)S(1)}, u32[]{:S(2)}, u32[]{:S(2)}) collective-permute-start(bf16[1024,256]{1,0:T(8,128)(2,1)} %get-tuple-element.102.c0.cot), channel_id=1, source_target_pairs={{0,1},{1,0},{2,3},{3,2},{4,5},{5,4},{6,7},{7,6},{8,9},{9,8},{10,11... | collective-permute-start | bytes 1572872 | tf_op jit(solution)/shard_map/ppermute | solution.py:666
  50.8 52.0 %collective-permute-start.5 = (bf16[1024,256]{1,0:T(8,128)(2,1)}, bf16[1024,256]{1,0:T(8,128)(2,1)S(1)}, u32[]{:S(2)}, u32[]{:S(2)}) collective-permute-start(bf16[1024,256]{1,0:T(8,128)(2,1)} %collective-permute-done.4.x2), channel_id=1, source_target_pairs={{0,1},{1,0},{2,3},{3,2},{4,5},{5,4},{6,7},{7,6},{8,9},{9,8},{10,11... | collective-permute-start | bytes 1572872 | tf_op jit(solution)/shard_map/ppermute | solution.py:666
  51.3 51.5 %collective-permute-start.8 = (bf16[1024,256]{1,0:T(8,128)(2,1)}, bf16[1024,256]{1,0:T(8,128)(2,1)S(1)}, u32[]{:S(2)}, u32[]{:S(2)}) collective-permute-start(bf16[1024,256]{1,0:T(8,128)(2,1)} %collective-permute-done.7.c2), channel_id=1, source_target_pairs={{0,1},{1,0},{2,3},{3,2},{4,5},{5,4},{6,7},{7,6},{8,9},{9,8},{10,11... | collective-permute-start | bytes 1572872 | tf_op jit(solution)/shard_map/ppermute | solution.py:666
  98.3 98.8 %collective-permute-start.25 = (f32[8,1024]{1,0:T(8,128)}, f32[8,1024]{1,0:T(8,128)S(1)}, u32[]{:S(2)}, u32[]{:S(2)}) collective-permute-start(f32[8,1024]{1,0:T(8,128)} %get-tuple-element.62), channel_id=1, source_target_pairs={{0,1},{1,0},{2,3},{3,2},{4,5},{5,4},{6,7},{7,6},{8,9},{9,8},{10,11... | collective-permute-start | bytes 98312 | tf_op jit(solution)/shard_map/ppermute | solution.py:666
  102.3 117.2 %collective-permute-start.23 = (bf16[2,1024,256]{2,1,0:T(8,128)(2,1)}, bf16[2,1024,256]{2,1,0:T(8,128)(2,1)S(1)}, u32[]{:S(2)}, u32[]{:S(2)}) collective-permute-start(bf16[2,1024,256]{2,1,0:T(8,128)(2,1)} %slice_bitcast_fusion.4), channel_id=1, source_target_pairs={{0,1},{1,0},{2,3},{3,2},{4,5},{5,4},{6,7},{7,6},{8,9},{9,8},{10,11... | collective-permute-start | bytes 3145736 | tf_op jit(solution)/shard_map/ppermute | solution.py:666
  102.5 118.5 %collective-permute-start.21 = (bf16[2,1024,256]{2,1,0:T(8,128)(2,1)}, bf16[2,1024,256]{2,1,0:T(8,128)(2,1)}, u32[]{:S(2)}, u32[]{:S(2)}) collective-permute-start(bf16[2,1024,256]{2,1,0:T(8,128)(2,1)} %slice_bitcast_fusion.5), channel_id=1, source_target_pairs={{0,1},{1,0},{2,3},{3,2},{4,5},{5,4},{6,7},{7,6},{8,9},{9,8},{10,11... | collective-permute-start | bytes 3145736 | tf_op jit(solution)/shard_map/ppermute | solution.py:666
  175.0 22.8 %collective-permute-start.13 = (f32[8,1024]{1,0:T(8,128)}, f32[8,1024]{1,0:T(8,128)S(1)}, u32[]{:S(2)}, u32[]{:S(2)}) collective-permute-start(f32[8,1024]{1,0:T(8,128)} %get-tuple-element.53), channel_id=1, source_target_pairs={{0,1},{1,0},{2,3},{3,2},{4,5},{5,4},{6,7},{7,6},{8,9},{9,8},{10,11... | collective-permute-start | bytes 98312 | tf_op jit(solution)/shard_map/ppermute | solution.py:666
  182.2 12.3 %collective-permute-start.33 = (bf16[4,128,256]{2,1,0:T(8,128)(2,1)S(1)}, bf16[4,128,256]{2,1,0:T(8,128)(2,1)S(1)}, u32[]{:S(2)}, u32[]{:S(2)}) collective-permute-start(bf16[4,128,256]{2,1,0:T(8,128)(2,1)S(1)} %slice_bitcast_fusion.18), channel_id=1, source_target_pairs={{0,4},{4,0},{8,12},{12,8},{16,20},{20,16},{24,28},{28,24},{1,5},{5... | collective-permute-start | bytes 786440 | tf_op jit(solution)/shard_map/ppermute | solution.py:666
  194.5 5.4 %collective-permute-start.34 = (bf16[2,128,256]{2,1,0:T(8,128)(2,1)S(1)}, bf16[2,128,256]{2,1,0:T(8,128)(2,1)S(1)}, u32[]{:S(2)}, u32[]{:S(2)}) collective-permute-start(bf16[2,128,256]{2,1,0:T(8,128)(2,1)S(1)} %slice.191), channel_id=1, source_target_pairs={{0,8},{4,12},{8,0},{12,4},{16,24},{20,28},{24,16},{28,20},{1,9},{5... | collective-permute-start | bytes 393224 | tf_op jit(solution)/shard_map/ppermute | solution.py:666
  197.1 20.8 %collective-permute-start.30 = (bf16[4,128,768]{2,1,0:T(8,128)(2,1)}, bf16[4,128,768]{2,1,0:T(8,128)(2,1)}, u32[]{:S(2)}, u32[]{:S(2)}) collective-permute-start(bf16[4,128,768]{2,1,0:T(8,128)(2,1)} %slice_bitcast_fusion.8), channel_id=1, source_target_pairs={{0,4},{4,0},{8,12},{12,8},{16,20},{20,16},{24,28},{28,24},{1,5},{5... | collective-permute-start | bytes 2359304 | tf_op jit(solution)/shard_map/ppermute | solution.py:666
  197.7 4.0 %collective-permute-start.26 = (f32[8,1024]{1,0:T(8,128)S(1)}, f32[8,1024]{1,0:T(8,128)S(1)}, u32[]{:S(2)}, u32[]{:S(2)}) collective-permute-start(f32[8,1024]{1,0:T(8,128)S(1)} %add.103), channel_id=1, source_target_pairs={{0,2},{1,3},{2,0},{3,1},{4,6},{5,7},{6,4},{7,5},{8,10},{9,11},{10,... | collective-permute-start | bytes 98312 | tf_op jit(solution)/shard_map/ppermute | solution.py:666
  200.0 3.9 %collective-permute-start.14 = (f32[8,1024]{1,0:T(8,128)S(1)}, f32[8,1024]{1,0:T(8,128)S(1)}, u32[]{:S(2)}, u32[]{:S(2)}) collective-permute-start(f32[8,1024]{1,0:T(8,128)S(1)} %add.98), channel_id=1, source_target_pairs={{0,2},{1,3},{2,0},{3,1},{4,6},{5,7},{6,4},{7,5},{8,10},{9,11},{10,... | collective-permute-start | bytes 98312 | tf_op jit(solution)/shard_map/ppermute | solution.py:666
  201.7 38.7 %collective-permute-start.39 = (bf16[4,128,1024]{2,1,0:T(8,128)(2,1)}, bf16[4,128,1024]{2,1,0:T(8,128)(2,1)}, u32[]{:S(2)}, u32[]{:S(2)}) collective-permute-start(bf16[4,128,1024]{2,1,0:T(8,128)(2,1)} %slice_bitcast_fusion), channel_id=1, source_target_pairs={{0,4},{4,0},{8,12},{12,8},{16,20},{20,16},{24,28},{28,24},{1,5},{5... | collective-permute-start | bytes 3145736 | tf_op jit(solution)/shard_map/ppermute | solution.py:666
  203.9 5.2 %collective-permute-start.35 = (bf16[128,256]{1,0:T(8,128)(2,1)S(1)}, bf16[128,256]{1,0:T(8,128)(2,1)S(1)}, u32[]{:S(2)}, u32[]{:S(2)}) collective-permute-start(bf16[128,256]{1,0:T(8,128)(2,1)S(1)} %slice_bitcast_fusion.22), channel_id=1, source_target_pairs={{0,16},{4,20},{8,24},{12,28},{16,0},{20,4},{24,8},{28,12},{1,17},{... | collective-permute-start | bytes 196616 | tf_op jit(solution)/shard_map/ppermute | solution.py:666
  209.1 52.6 %collective-permute-start.36 = (bf16[4,128,1024]{2,1,0:T(8,128)(2,1)}, bf16[4,128,1024]{2,1,0:T(8,128)(2,1)}, u32[]{:S(2)}, u32[]{:S(2)}) collective-permute-start(bf16[4,128,1024]{2,1,0:T(8,128)(2,1)} %slice_bitcast_fusion.2), channel_id=1, source_target_pairs={{0,4},{4,0},{8,12},{12,8},{16,20},{20,16},{24,28},{28,24},{1,5},{5... | collective-permute-start | bytes 3145736 | tf_op jit(solution)/shard_map/ppermute | solution.py:666
  218.0 48.4 %collective-permute-start.11 = (bf16[2,1024,256]{2,1,0:T(8,128)(2,1)}, bf16[2,1024,256]{2,1,0:T(8,128)(2,1)S(1)}, u32[]{:S(2)}, u32[]{:S(2)}) collective-permute-start(bf16[2,1024,256]{2,1,0:T(8,128)(2,1)} %slice_bitcast_fusion.6), channel_id=1, source_target_pairs={{0,1},{1,0},{2,3},{3,2},{4,5},{5,4},{6,7},{7,6},{8,9},{9,8},{10,11... | collective-permute-start | bytes 3145736 | tf_op jit(solution)/shard_map/ppermute | solution.py:666
  219.4 22.7 %copy-start.8 = (bf16[2,4,128,1024]{3,2,1,0:T(8,128)(2,1)S(1)}, bf16[2,4,128,1024]{3,2,1,0:T(8,128)(2,1)}, u32[]{:S(2)}) copy-start(bf16[2,4,128,1024]{3,2,1,0:T(8,128)(2,1)} %weight_grad.7) | copy-start | bytes 6291460
  219.5 24.0 %copy-start.3 = (bf16[2,1024,256]{2,1,0:T(8,128)(2,1)}, bf16[2,1024,256]{2,1,0:T(8,128)(2,1)S(1)}, u32[]{:S(2)}) copy-start(bf16[2,1024,256]{2,1,0:T(8,128)(2,1)S(1)} %collective-permute-done.23.core_g) | copy-start | bytes 3145732
  219.5 49.5 %collective-permute-start.9 = (bf16[2,1024,256]{2,1,0:T(8,128)(2,1)S(1)}, bf16[2,1024,256]{2,1,0:T(8,128)(2,1)S(1)}, u32[]{:S(2)}, u32[]{:S(2)}) collective-permute-start(bf16[2,1024,256]{2,1,0:T(8,128)(2,1)S(1)} %copy-done.14), channel_id=1, source_target_pairs={{0,1},{1,0},{2,3},{3,2},{4,5},{5,4},{6,7},{7,6},{8,9},{9,8},{10,11... | collective-permute-start | bytes 3145736 | tf_op jit(solution)/shard_map/ppermute | solution.py:666
  220.9 42.4 %copy-start.7 = (bf16[2,4,128,1024]{3,2,1,0:T(8,128)(2,1)S(1)}, bf16[2,4,128,1024]{3,2,1,0:T(8,128)(2,1)}, u32[]{:S(2)}) copy-start(bf16[2,4,128,1024]{3,2,1,0:T(8,128)(2,1)} %weight_grad.6) | copy-start | bytes 6291460
  221.0 47.5 %collective-permute-start.31 = (bf16[2,128,768]{2,1,0:T(8,128)(2,1)S(1)}, bf16[2,128,768]{2,1,0:T(8,128)(2,1)S(1)}, u32[]{:S(2)}, u32[]{:S(2)}) collective-permute-start(bf16[2,128,768]{2,1,0:T(8,128)(2,1)S(1)} %slice.185), channel_id=1, source_target_pairs={{0,8},{4,12},{8,0},{12,4},{16,24},{20,28},{24,16},{28,20},{1,9},{5... | collective-permute-start | bytes 1179656 | tf_op jit(solution)/shard_map/ppermute | solution.py:666
  240.4 48.0 %collective-permute-start.24 = (bf16[1024,256]{1,0:T(8,128)(2,1)}, bf16[1024,256]{1,0:T(8,128)(2,1)}, u32[]{:S(2)}, u32[]{:S(2)}) collective-permute-start(bf16[1024,256]{1,0:T(8,128)(2,1)} %fusion.3), channel_id=1, source_target_pairs={{0,2},{1,3},{2,0},{3,1},{4,6},{5,7},{6,4},{7,5},{8,10},{9,11},{10,... | collective-permute-start | bytes 1572872 | tf_op jit(solution)/shard_map/ppermute | solution.py:666
  261.6 26.8 %collective-permute-start.22 = (bf16[1024,256]{1,0:T(8,128)(2,1)}, bf16[1024,256]{1,0:T(8,128)(2,1)}, u32[]{:S(2)}, u32[]{:S(2)}) collective-permute-start(bf16[1024,256]{1,0:T(8,128)(2,1)} %fusion.4), channel_id=1, source_target_pairs={{0,2},{1,3},{2,0},{3,1},{4,6},{5,7},{6,4},{7,5},{8,10},{9,11},{10,... | collective-permute-start | bytes 1572872 | tf_op jit(solution)/shard_map/ppermute | solution.py:666
  266.4 17.1 %collective-permute-start.40 = (bf16[2,128,1024]{2,1,0:T(8,128)(2,1)}, bf16[2,128,1024]{2,1,0:T(8,128)(2,1)}, u32[]{:S(2)}, u32[]{:S(2)}) collective-permute-start(bf16[2,128,1024]{2,1,0:T(8,128)(2,1)} %slice.204), channel_id=1, source_target_pairs={{0,8},{4,12},{8,0},{12,4},{16,24},{20,28},{24,16},{28,20},{1,9},{5... | collective-permute-start | bytes 1572872 | tf_op jit(solution)/shard_map/ppermute | solution.py:666
  268.5 24.8 %collective-permute-start.12 = (bf16[1024,256]{1,0:T(8,128)(2,1)S(1)}, bf16[1024,256]{1,0:T(8,128)(2,1)}, u32[]{:S(2)}, u32[]{:S(2)}) collective-permute-start(bf16[1024,256]{1,0:T(8,128)(2,1)S(1)} %fusion.5), channel_id=1, source_target_pairs={{0,2},{1,3},{2,0},{3,1},{4,6},{5,7},{6,4},{7,5},{8,10},{9,11},{10,... | collective-permute-start | bytes 1572872 | tf_op jit(solution)/shard_map/ppermute | solution.py:666
  269.0 13.0 %collective-permute-start.32 = (bf16[128,768]{1,0:T(8,128)(2,1)S(1)}, bf16[128,768]{1,0:T(8,128)(2,1)S(1)}, u32[]{:S(2)}, u32[]{:S(2)}) collective-permute-start(bf16[128,768]{1,0:T(8,128)(2,1)S(1)} %slice_bitcast_fusion.20), channel_id=1, source_target_pairs={{0,16},{4,20},{8,24},{12,28},{16,0},{20,4},{24,8},{28,12},{1,17},{... | collective-permute-start | bytes 589832 | tf_op jit(solution)/shard_map/ppermute | solution.py:666
  282.0 15.1 %collective-permute-start.10 = (bf16[1024,256]{1,0:T(8,128)(2,1)}, bf16[1024,256]{1,0:T(8,128)(2,1)}, u32[]{:S(2)}, u32[]{:S(2)}) collective-permute-start(bf16[1024,256]{1,0:T(8,128)(2,1)} %fusion.6), channel_id=1, source_target_pairs={{0,2},{1,3},{2,0},{3,1},{4,6},{5,7},{6,4},{7,5},{8,10},{9,11},{10,... | collective-permute-start | bytes 1572872 | tf_op jit(solution)/shard_map/ppermute | solution.py:666
  283.5 20.0 %collective-permute-start.37 = (bf16[2,128,1024]{2,1,0:T(8,128)(2,1)}, bf16[2,128,1024]{2,1,0:T(8,128)(2,1)S(1)}, u32[]{:S(2)}, u32[]{:S(2)}) collective-permute-start(bf16[2,128,1024]{2,1,0:T(8,128)(2,1)} %slice.197), channel_id=1, source_target_pairs={{0,8},{4,12},{8,0},{12,4},{16,24},{20,28},{24,16},{28,20},{1,9},{5... | collective-permute-start | bytes 1572872 | tf_op jit(solution)/shard_map/ppermute | solution.py:666
  288.4 29.2 %collective-permute-start.41 = (bf16[128,1024]{1,0:T(8,128)(2,1)S(1)}, bf16[128,1024]{1,0:T(8,128)(2,1)S(1)}, u32[]{:S(2)}, u32[]{:S(2)}) collective-permute-start(bf16[128,1024]{1,0:T(8,128)(2,1)S(1)} %slice_bitcast_fusion.14), channel_id=1, source_target_pairs={{0,16},{4,20},{8,24},{12,28},{16,0},{20,4},{24,8},{28,12},{1,17},{... | collective-permute-start | bytes 786440 | tf_op jit(solution)/shard_map/ppermute | solution.py:666
  302.9 3.7 %collective-permute-start.27 = (f32[1792]{0:T(1024)S(1)}, f32[1792]{0:T(1024)S(1)}, u32[]{:S(2)}, u32[]{:S(2)}) collective-permute-start(f32[1792]{0:T(1024)S(1)} %pad_maximum_fusion.2), channel_id=1, source_target_pairs={{0,4},{4,0},{8,12},{12,8},{16,20},{20,16},{24,28},{28,24},{1,5},{5... | collective-permute-start | bytes 21512 | tf_op jit(solution)/shard_map/ppermute | solution.py:666
  303.6 15.1 %collective-permute-start.38 = (bf16[128,1024]{1,0:T(8,128)(2,1)S(1)}, bf16[128,1024]{1,0:T(8,128)(2,1)S(1)}, u32[]{:S(2)}, u32[]{:S(2)}) collective-permute-start(bf16[128,1024]{1,0:T(8,128)(2,1)S(1)} %slice_bitcast_fusion.16), channel_id=1, source_target_pairs={{0,16},{4,20},{8,24},{12,28},{16,0},{20,4},{24,8},{28,12},{1,17},{... | collective-permute-start | bytes 786440 | tf_op jit(solution)/shard_map/ppermute | solution.py:666
  306.6 3.7 %collective-permute-start.28 = (f32[1792]{0:T(1024)S(1)}, f32[1792]{0:T(1024)S(1)}, u32[]{:S(2)}, u32[]{:S(2)}) collective-permute-start(f32[1792]{0:T(1024)S(1)} %fusion.10), channel_id=1, source_target_pairs={{0,8},{4,12},{8,0},{12,4},{16,24},{20,28},{24,16},{28,20},{1,9},{5... | collective-permute-start | bytes 21512 | tf_op jit(solution)/shard_map/ppermute | solution.py:666
  310.3 6.1 %collective-permute-start.29 = (f32[1792]{0:T(1024)S(1)}, f32[1792]{0:T(1024)S(1)}, u32[]{:S(2)}, u32[]{:S(2)}) collective-permute-start(f32[1792]{0:T(1024)S(1)} %add.110), channel_id=1, source_target_pairs={{0,16},{4,20},{8,24},{12,28},{16,0},{20,4},{24,8},{28,12},{1,17},{... | collective-permute-start | bytes 21512 | tf_op jit(solution)/shard_map/ppermute | solution.py:666
  (28 other events, 175.1 us)
